TPU v7x, 32 devices: a whole 2x2x4 slice. The times are simulated.
32 devices in a mesh: shard: 2 (over y), rep: 16 (over z, x, core).
Axes of the slice: x: 2, y: 2, z: 4, core: 2. Of those that a mesh axis runs over, the one named last changes fastest.
Arguments:
- tokens: bfloat16 [32768, 768], P(('shard', 'rep')), may hold values from -6 to 6
- lengths: int32 [32], P(('shard', 'rep')), may hold values from 513 to 1024, as said below
- cotangent: bfloat16 [32768, 768], P(('shard', 'rep')), may hold values from -6 to 6
- gain_one: bfloat16 [768], P('shard'), may hold values from 0.25 to 1.75
- shift_one: bfloat16 [768], P('shard'), may hold values from -3 to 3
- attend_weight: bfloat16 [768, 2304], P('shard'), may hold values from -0.375 to 0.375
- attend_bias: bfloat16 [1536], P('shard'), may hold values from -0.29882812 to 0.29882812
- mixing_weight: bfloat16 [768, 768], P('shard'), may hold values from -0.21875 to 0.21875
- mixing_bias: bfloat16 [768], P('shard'), may hold values from -3 to 3
- gain_two: bfloat16 [768], P('shard'), may hold values from 0.25 to 1.75
- shift_two: bfloat16 [768], P('shard'), may hold values from -3 to 3
- expand_weight: bfloat16 [768, 3072], P('shard'), may hold values from -0.21875 to 0.21875
- expand_bias: bfloat16 [3072], P('shard'), may hold values from -3 to 3
- reduce_weight: bfloat16 [3072, 768], P('shard'), may hold values from -0.109375 to 0.109375
- reduce_bias: bfloat16 [768], P('shard'), may hold values from -3 to 3
Outputs:
- block_output: bfloat16 [32768, 768], P(('shard', 'rep'))
- tokens_slope: bfloat16 [32768, 768], P(('shard', 'rep'))
- gain_one_slope: float32 [768], P('shard')
- shift_one_slope: float32 [768], P('shard')
- attend_weight_slope: float32 [768, 2304], P('shard')
- attend_bias_slope: float32 [1536], P('shard')
- mixing_weight_slope: float32 [768, 768], P('shard')
- mixing_bias_slope: float32 [768], P('shard')
- gain_two_slope: float32 [768], P('shard')
- shift_two_slope: float32 [768], P('shard')
- expand_weight_slope: float32 [768, 3072], P('shard')
- expand_bias_slope: float32 [3072], P('shard')
- reduce_weight_slope: float32 [3072, 768], P('shard')
- reduce_bias_slope: float32 [768], P('shard')
Inputs may be any that keep to these rules, and one draw needn't show every extreme that they name: `lengths`: each sequence's real tokens fill the front of its 1024 slots, more than half of them; the rest are padding.
All inputs are finite; a program needn't handle non-finite values.
Results may differ from a plain program's by a relative error of at most 0.02.
Values may be sent and summed in bfloat16 or wider, within the bound.
A program may use at most 256 MiB of HBM per device.

v0:
```python
import jax
import jax.numpy as jnp
from jax import lax
from jax.sharding import PartitionSpec as P

D = 768
H = 12
HD = 64
SEQ = 1024


def normalize(values, gain, shift):
    center = values - jnp.mean(values, axis=-1, keepdims=True)
    spread = lax.rsqrt(jnp.mean(center * center, axis=-1, keepdims=True) + 1e-05)
    normed = center * spread
    return (normed * gain + shift, normed, spread)


def normalize_back(upstream, normed, spread, gain):
    scaled = upstream * gain
    centered = scaled - jnp.mean(scaled, axis=-1, keepdims=True)
    return spread * (centered - normed * jnp.mean(scaled * normed, axis=-1, keepdims=True))


def block_scores(piece, keys, length):
    scale = 1.0 / HD**0.5
    keyvalid = lax.iota(jnp.int32, keys.shape[0]) < length
    scores = jnp.einsum("qhd,khd->hqk", piece, keys, preferred_element_type=jnp.float32) * scale
    return jnp.where(keyvalid[None, None, :], scores, -1e30)


def attend_sequence(item):
    query, keys, values, length = item
    block = min(512, SEQ)
    count = SEQ // block

    def one_block(piece):
        scores = block_scores(piece, keys, length)
        peak = jnp.max(scores, axis=-1, keepdims=True)
        expo = jnp.exp(scores - peak)
        total = jnp.sum(expo, axis=-1, keepdims=True)
        probs = (expo / total).astype(jnp.bfloat16)
        mixed = jnp.einsum("hqk,khd->qhd", probs, values, preferred_element_type=jnp.float32)
        return (mixed, (peak + jnp.log(total))[..., 0])

    mixed, logsum = lax.map(one_block, query.reshape(count, block, H, HD))
    return (mixed.reshape(SEQ, H, HD), logsum)


def attend_backward(item):
    query, keys, values, length, logsum, upstream = item
    block = min(512, SEQ)
    count = SEQ // block
    scale = 1.0 / HD**0.5

    def one_block(carry, inputs):
        piece, block_sum, block_grad = inputs
        scores = block_scores(piece, keys, length)
        probs = jnp.exp(scores - block_sum[..., None])
        dprobs = jnp.einsum("qhd,khd->hqk", block_grad, values, preferred_element_type=jnp.float32)
        delta = jnp.sum(probs * dprobs, axis=-1, keepdims=True)
        dscores = (probs * (dprobs - delta)).astype(jnp.bfloat16)
        dquery = (
            jnp.einsum("hqk,khd->qhd", dscores, keys, preferred_element_type=jnp.float32) * scale
        )
        dkeys = (
            carry[0]
            + jnp.einsum("hqk,qhd->khd", dscores, piece, preferred_element_type=jnp.float32) * scale
        )
        dvalues = carry[1] + jnp.einsum(
            "hqk,qhd->khd",
            probs.astype(jnp.bfloat16),
            block_grad,
            preferred_element_type=jnp.float32,
        )
        return ((dkeys, dvalues), dquery)

    initial = (jnp.zeros((SEQ, H, HD), jnp.float32), jnp.zeros((SEQ, H, HD), jnp.float32))
    pieces = (query.reshape(count, block, H, HD), logsum, upstream.reshape(count, block, H, HD))
    (dkeys, dvalues), dquery = lax.scan(one_block, initial, pieces)
    return (dquery.reshape(SEQ, H, HD), dkeys, dvalues)


def column_sums(values):
    return jnp.sum(values.astype(jnp.float32), axis=0)


def shards(
    tokens,
    lengths,
    cotangent,
    gain_one,
    shift_one,
    attend_weight,
    attend_bias,
    mixing_weight,
    mixing_bias,
    gain_two,
    shift_two,
    expand_weight,
    expand_bias,
    reduce_weight,
    reduce_bias,
):
    gathered = (
        lax.all_gather(gain_one, "shard", axis=0, tiled=True),
        lax.all_gather(shift_one, "shard", axis=0, tiled=True),
        lax.all_gather(attend_weight, "shard", axis=0, tiled=True),
        lax.all_gather(attend_bias, "shard", axis=0, tiled=True),
        lax.all_gather(mixing_weight, "shard", axis=0, tiled=True),
        lax.all_gather(mixing_bias, "shard", axis=0, tiled=True),
        lax.all_gather(gain_two, "shard", axis=0, tiled=True),
        lax.all_gather(shift_two, "shard", axis=0, tiled=True),
        lax.all_gather(expand_weight, "shard", axis=0, tiled=True),
        lax.all_gather(expand_bias, "shard", axis=0, tiled=True),
        lax.all_gather(reduce_weight, "shard", axis=0, tiled=True),
        lax.all_gather(reduce_bias, "shard", axis=0, tiled=True),
    )
    inputs = tokens.astype(jnp.float32)
    total_rows = inputs.shape[0]
    seqcount = total_rows // SEQ
    position = lax.iota(jnp.int32, SEQ)
    live = (position[None, :] < lengths[:, None]).reshape(total_rows, 1).astype(jnp.float32)
    gain_first = gathered[0].astype(jnp.float32)
    shift_first = gathered[1].astype(jnp.float32)
    bias_attend = gathered[3].astype(jnp.float32)
    bias_mixing = gathered[5].astype(jnp.float32)
    gain_second = gathered[6].astype(jnp.float32)
    shift_second = gathered[7].astype(jnp.float32)
    bias_expand = gathered[9].astype(jnp.float32)
    bias_reduce = gathered[11].astype(jnp.float32)
    normed_in, norm_one, spread_one = normalize(inputs, gain_first, shift_first)
    first_low = normed_in.astype(jnp.bfloat16)
    zeros = jnp.zeros((D,), jnp.float32)
    full_bias = jnp.concatenate([bias_attend[:D], zeros, bias_attend[D:]])
    mixed_rows = jnp.dot(first_low, gathered[2], preferred_element_type=jnp.float32) + full_bias
    query = mixed_rows[:, :D].astype(jnp.bfloat16).reshape(seqcount, SEQ, H, HD)
    keys = mixed_rows[:, D : 2 * D].astype(jnp.bfloat16).reshape(seqcount, SEQ, H, HD)
    values = mixed_rows[:, 2 * D :].astype(jnp.bfloat16).reshape(seqcount, SEQ, H, HD)
    attended, logsum = lax.map(attend_sequence, (query, keys, values, lengths))
    attended_low = attended.reshape(total_rows, D).astype(jnp.bfloat16)
    branch = jnp.dot(attended_low, gathered[4], preferred_element_type=jnp.float32) + bias_mixing
    middle = inputs + branch
    normed_mid, norm_two, spread_two = normalize(middle, gain_second, shift_second)
    second_low = normed_mid.astype(jnp.bfloat16)
    hidden = jnp.dot(second_low, gathered[8], preferred_element_type=jnp.float32) + bias_expand
    sigma = jax.nn.sigmoid(1.702 * hidden)
    active_low = (hidden * sigma).astype(jnp.bfloat16)
    final = jnp.dot(active_low, gathered[10], preferred_element_type=jnp.float32) + bias_reduce
    block_output = (live * (middle + final)).astype(jnp.bfloat16)
    upstream = cotangent.astype(jnp.float32) * live
    up_low = upstream.astype(jnp.bfloat16)
    reduce_bias_slope = column_sums(up_low)
    reduce_weight_slope = jnp.dot(active_low.T, up_low, preferred_element_type=jnp.float32)
    d_active = jnp.dot(up_low, gathered[10].T, preferred_element_type=jnp.float32)
    hidden_low = (d_active * (sigma + 1.702 * hidden * sigma * (1.0 - sigma))).astype(jnp.bfloat16)
    expand_bias_slope = column_sums(hidden_low)
    expand_weight_slope = jnp.dot(second_low.T, hidden_low, preferred_element_type=jnp.float32)
    d_second = jnp.dot(hidden_low, gathered[8].T, preferred_element_type=jnp.float32)
    gain_two_slope = jnp.sum(d_second * norm_two, axis=0)
    shift_two_slope = jnp.sum(d_second, axis=0)
    d_middle = upstream + normalize_back(
        d_second, norm_two, spread_two, gathered[6].astype(jnp.float32)
    )
    middle_low = d_middle.astype(jnp.bfloat16)
    mixing_bias_slope = column_sums(middle_low)
    mixing_weight_slope = jnp.dot(attended_low.T, middle_low, preferred_element_type=jnp.float32)
    d_attended = jnp.dot(middle_low, gathered[4].T, preferred_element_type=jnp.float32)
    d_attended = d_attended.astype(jnp.bfloat16).reshape(seqcount, SEQ, H, HD)
    dquery, dkeys, dvalues = lax.map(
        attend_backward, (query, keys, values, lengths, logsum, d_attended)
    )
    d_mixed = jnp.concatenate(
        [
            dquery.reshape(total_rows, D),
            dkeys.reshape(total_rows, D),
            dvalues.reshape(total_rows, D),
        ],
        axis=1,
    ).astype(jnp.bfloat16)
    mixed_sums = column_sums(d_mixed)
    attend_bias_slope = jnp.concatenate([mixed_sums[:D], mixed_sums[2 * D :]])
    attend_weight_slope = jnp.dot(first_low.T, d_mixed, preferred_element_type=jnp.float32)
    d_first = jnp.dot(d_mixed, gathered[2].T, preferred_element_type=jnp.float32)
    gain_one_slope = jnp.sum(d_first * norm_one, axis=0)
    shift_one_slope = jnp.sum(d_first, axis=0)
    d_inputs = d_middle + normalize_back(
        d_first, norm_one, spread_one, gathered[0].astype(jnp.float32)
    )
    tokens_slope = d_inputs.astype(jnp.bfloat16)
    owned = (
        lax.psum_scatter(
            gain_one_slope.astype(jnp.bfloat16), "shard", scatter_dimension=0, tiled=True
        ).astype(jnp.float32),
        lax.psum_scatter(
            shift_one_slope.astype(jnp.bfloat16), "shard", scatter_dimension=0, tiled=True
        ).astype(jnp.float32),
        lax.psum_scatter(
            attend_weight_slope.astype(jnp.bfloat16), "shard", scatter_dimension=0, tiled=True
        ).astype(jnp.float32),
        lax.psum_scatter(
            attend_bias_slope.astype(jnp.bfloat16), "shard", scatter_dimension=0, tiled=True
        ).astype(jnp.float32),
        lax.psum_scatter(
            mixing_weight_slope.astype(jnp.bfloat16), "shard", scatter_dimension=0, tiled=True
        ).astype(jnp.float32),
        lax.psum_scatter(
            mixing_bias_slope.astype(jnp.bfloat16), "shard", scatter_dimension=0, tiled=True
        ).astype(jnp.float32),
        lax.psum_scatter(
            gain_two_slope.astype(jnp.bfloat16), "shard", scatter_dimension=0, tiled=True
        ).astype(jnp.float32),
        lax.psum_scatter(
            shift_two_slope.astype(jnp.bfloat16), "shard", scatter_dimension=0, tiled=True
        ).astype(jnp.float32),
        lax.psum_scatter(
            expand_weight_slope.astype(jnp.bfloat16), "shard", scatter_dimension=0, tiled=True
        ).astype(jnp.float32),
        lax.psum_scatter(
            expand_bias_slope.astype(jnp.bfloat16), "shard", scatter_dimension=0, tiled=True
        ).astype(jnp.float32),
        lax.psum_scatter(
            reduce_weight_slope.astype(jnp.bfloat16), "shard", scatter_dimension=0, tiled=True
        ).astype(jnp.float32),
        lax.psum_scatter(
            reduce_bias_slope.astype(jnp.bfloat16), "shard", scatter_dimension=0, tiled=True
        ).astype(jnp.float32),
    )
    summed = (
        lax.psum(owned[0].astype(jnp.bfloat16), "rep").astype(jnp.float32),
        lax.psum(owned[1].astype(jnp.bfloat16), "rep").astype(jnp.float32),
        lax.psum(owned[2].astype(jnp.bfloat16), "rep").astype(jnp.float32),
        lax.psum(owned[3].astype(jnp.bfloat16), "rep").astype(jnp.float32),
        lax.psum(owned[4].astype(jnp.bfloat16), "rep").astype(jnp.float32),
        lax.psum(owned[5].astype(jnp.bfloat16), "rep").astype(jnp.float32),
        lax.psum(owned[6].astype(jnp.bfloat16), "rep").astype(jnp.float32),
        lax.psum(owned[7].astype(jnp.bfloat16), "rep").astype(jnp.float32),
        lax.psum(owned[8].astype(jnp.bfloat16), "rep").astype(jnp.float32),
        lax.psum(owned[9].astype(jnp.bfloat16), "rep").astype(jnp.float32),
        lax.psum(owned[10].astype(jnp.bfloat16), "rep").astype(jnp.float32),
        lax.psum(owned[11].astype(jnp.bfloat16), "rep").astype(jnp.float32),
    )
    return (
        block_output,
        tokens_slope,
        summed[0],
        summed[1],
        summed[2],
        summed[3],
        summed[4],
        summed[5],
        summed[6],
        summed[7],
        summed[8],
        summed[9],
        summed[10],
        summed[11],
    )


def solution(mesh):
    in_specs = (
        P(("shard", "rep"), None),
        P(("shard", "rep")),
        P(("shard", "rep"), None),
        P("shard"),
        P("shard"),
        P("shard", None),
        P("shard"),
        P("shard", None),
        P("shard"),
        P("shard"),
        P("shard"),
        P("shard", None),
        P("shard"),
        P("shard", None),
        P("shard"),
    )
    out_specs = (
        P(("shard", "rep"), None),
        P(("shard", "rep"), None),
        P("shard"),
        P("shard"),
        P("shard", None),
        P("shard"),
        P("shard", None),
        P("shard"),
        P("shard"),
        P("shard"),
        P("shard", None),
        P("shard"),
        P("shard", None),
        P("shard"),
    )
    return jax.shard_map(shards, mesh=mesh, in_specs=in_specs, out_specs=out_specs, check_vma=False)
```

profile of v0, /device:TPU:0, one launch (start us, length us, event | category | flops | bytes accessed | tf_op | source)
XLA Modules:
  0.0 792.6 jit_solution(16247023017070913006)
XLA Ops:
  10.8 5.2 all-gather
  16.1 4.3 all-gather.1
  20.5 4.3 all-gather.3
  25.5 4.3 all-gather.4
  30.4 4.3 all-gather.5
  35.4 4.4 all-gather.2
  40.4 4.5 all-gather.6
  49.9 12.1 %all-gather.13.cloned.1.call-done = bf16[768,2304]{1,0:T(8,128)(2,1)} async-done(((bf16[384,2304]{1,0:T(8,128)(2,1)}), bf16[768,2304]{1,0:T(8,128)(2,1)}) %all-gather.13.cloned.1.call-update) | async-done | bytes 3538960 | tf_op jit(solution)/shard_map/all_gather | solution.py:108
  62.0 6.4 add_convert_fusion
  75.0 3.8 reshape.170
  81.8 71.3 %while.47 = (s32[]{:T(128)}, bf16[2,512,12,64]{1,3,2,0:T(8,128)(2,1)}, f32[2,12,512]{2,1,0:T(8,128)S(1)}, s32[]{:T(128)}, bf16[2,512,12,64]{1,3,2,0:T(8,128)(2,1...) while((s32[]{:T(128)}, bf16[2,512,12,64]{1,3,2,0:T(8,128)(2,1)}, ...), condition=%wide.region_5.6_spmd, body=%wide.region_2.5_spmd.sunk | while | flops 1686105088 | bytes 100118728 | solution.py:46
  82.5 10.1 %fusion.101 = (f32[12,512]{1,0:T(8,128)S(1)}, f32[12,512,1024]{2,1,0:T(8,128)}) fusion(pred[1024]{0:T(1024)(128)(4,1)S(1)} %iota_compare_fusion.5, bf16[1024,12,64]{0,2,1:T(8,128)(2,1)S(1)} %get-tuple-element.507, bf16[2,512,12,64]{1,3,2,0:T(8,128)(2,1)S(1)} %get-tuple-element.506, s32[]{:T(128)S(6)} %copy.90), kind=kOutput, calls=%fused_computation.3.clone.1 | convolution fusion | flops 824174592 | bytes 27550724 | tf_op jit(solution)/shard_map/while/body/eval_jaxpr/while/body/eval_jaxpr/qhd,khd->hqk/dot_general | solution.py:28
  92.6 13.4 %fusion.102 = f32[12,512]{1,0:T(8,128)S(1)} fusion(f32[12,512,1024]{2,1,0:T(8,128)} %get-tuple-element.472, f32[12,512]{1,0:T(8,128)S(1)} %get-tuple-element.473, pred[1024]{0:T(1024)(128)(4,1)S(1)} %iota_compare_fusion.5), kind=kLoop, calls=%fused_computation.4.clone.1 | loop fusion | flops 25159680 | bytes 25216000 | tf_op jit(solution)/shard_map/while/body/eval_jaxpr/while/body/eval_jaxpr/reduce_sum | solution.py:41
  106.1 11.2 %bitcast_dynamic-update-slice_fusion.6 = bf16[2,512,12,64]{1,3,2,0:T(8,128)(2,1)S(1)} fusion(bf16[2,512,12,64]{1,3,2,0:T(8,128)(2,1)S(1)} %copy-done.12, s32[]{:T(128)S(6)} %copy.90, bf16[1024,12,64]{0,2,1:T(8,128)(2,1)S(1)} %copy-done.1, f32[12,512,1024]{2,1,0:T(8,128)} %get-tuple-element.472, f32[12,512]{1,0:T(8,128)S(1)} %fusion.102, ...), kind=kOutput, calls=%fused_computation.6.clone.1 | convolution fusion | flops 836763648 | bytes 28378116 | tf_op jit(solution)/shard_map/while/body/eval_jaxpr/while/body/eval_jaxpr/hqk,khd->qhd/dot_general | solution.py:43
  119.1 10.1 %fusion.101 = (f32[12,512]{1,0:T(8,128)S(1)}, f32[12,512,1024]{2,1,0:T(8,128)}) fusion(pred[1024]{0:T(1024)(128)(4,1)S(1)} %iota_compare_fusion.5, bf16[1024,12,64]{0,2,1:T(8,128)(2,1)S(1)} %get-tuple-element.507, bf16[2,512,12,64]{1,3,2,0:T(8,128)(2,1)S(1)} %get-tuple-element.506, s32[]{:T(128)S(6)} %copy.90), kind=kOutput, calls=%fused_computation.3.clone.1 | convolution fusion | flops 824174592 | bytes 27550724 | tf_op jit(solution)/shard_map/while/body/eval_jaxpr/while/body/eval_jaxpr/qhd,khd->hqk/dot_general | solution.py:28
  129.2 11.4 %fusion.102 = f32[12,512]{1,0:T(8,128)S(1)} fusion(f32[12,512,1024]{2,1,0:T(8,128)} %get-tuple-element.472, f32[12,512]{1,0:T(8,128)S(1)} %get-tuple-element.473, pred[1024]{0:T(1024)(128)(4,1)S(1)} %iota_compare_fusion.5), kind=kLoop, calls=%fused_computation.4.clone.1 | loop fusion | flops 25159680 | bytes 25216000 | tf_op jit(solution)/shard_map/while/body/eval_jaxpr/while/body/eval_jaxpr/reduce_sum | solution.py:41
  140.6 11.2 %bitcast_dynamic-update-slice_fusion.6 = bf16[2,512,12,64]{1,3,2,0:T(8,128)(2,1)S(1)} fusion(bf16[2,512,12,64]{1,3,2,0:T(8,128)(2,1)S(1)} %copy-done.12, s32[]{:T(128)S(6)} %copy.90, bf16[1024,12,64]{0,2,1:T(8,128)(2,1)S(1)} %copy-done.1, f32[12,512,1024]{2,1,0:T(8,128)} %get-tuple-element.472, f32[12,512]{1,0:T(8,128)S(1)} %fusion.102, ...), kind=kOutput, calls=%fused_computation.6.clone.1 | convolution fusion | flops 836763648 | bytes 28378116 | tf_op jit(solution)/shard_map/while/body/eval_jaxpr/while/body/eval_jaxpr/hqk,khd->qhd/dot_general | solution.py:43
  153.1 3.0 copy.68
  157.7 4.5 fusion.60
  164.4 14.5 %multiply_convert_fusion.2 = (bf16[1024,3072]{1,0:T(8,128)(2,1)}, f32[1024,3072]{1,0:T(8,128)}) fusion(f32[3072]{0:T(1024)S(1)} %bitcast.127, bf16[768,3072]{1,0:T(8,128)(2,1)} %all-gather.17.cloned.1.call-done, f32[1024,768]{0,1:T(8,128)} %copy-done.4, f32[768]{0:T(1024)S(1)} %copy-done.38, f32[768]{0:T(1024)S(1)} %copy-done.25, ...), kind=kOutput, calls=%fused_computation.43 | convolution fusion | flops 4857790464 | bytes 26765312 | tf_op jit(solution)/shard_map/dot_general | solution.py:146
  178.9 35.8 %all-gather.19.cloned.1.call-done = bf16[3072,768]{1,0:T(8,128)(2,1)} async-done(((bf16[1536,768]{1,0:T(8,128)(2,1)}), bf16[3072,768]{1,0:T(8,128)(2,1)}) %all-gather.19.cloned.1.call-update) | async-done | bytes 4718608 | tf_op jit(solution)/shard_map/all_gather | solution.py:116
  214.7 13.9 %fusion.63 = (bf16[3072]{0:T(1024)(128)(2,1)}, bf16[1024,3072]{1,0:T(8,128)(2,1)S(1)}) fusion(f32[1024,3072]{1,0:T(8,128)} %get-tuple-element.365, f32[3072]{0:T(1024)S(1)} %bitcast.128, bf16[3072,768]{1,0:T(8,128)(2,1)} %all-gather.19.cloned.1.call-done, bf16[1024,768]{0,1:T(8,128)(2,1)} %copy.70, f32[1024]{0:T(1024)S(1)} %copy-done.31), kind=kOutput, calls=%fused_computation.113 | convolution fusion | flops 4871943168 | bytes 25188352 | tf_op jit(solution)/shard_map/dot_general | solution.py:155
  228.6 7.3 fusion.62
  235.9 3.5 copy.71
  239.4 4.6 multiply_reduce_fusion.1
  244.1 3.8 convert_reduce_fusion.7
  252.2 4.8 convolution_convert_fusion.3
  257.1 2.7 copy.72
  259.7 3.8 reshape.171
  263.6 2.9 copy.74
  267.8 163.4 %while.48 = (s32[]{:T(128)}, f32[1024,12,64]{0,2,1:T(8,128)}, f32[1024,12,64]{0,2,1:T(8,128)}, bf16[2,512,12,64]{1,3,2,0:T(8,128)(2,1)}, bf16[2,512,12,64]{1,3,2...) while((s32[]{:T(128)}, f32[1024,12,64]{0,2,1:T(8,128)}, ...), condition=%wide.region_12.13_spmd.clone, body=%wide.region_10.12_spmd.clone.sunk | while | flops 4125223936 | bytes 217239728 | solution.py:80
  268.6 10.1 %fusion.112 = f32[12,512,1024]{2,1,0:T(8,128)} fusion(bf16[1024,12,64]{0,2,1:T(8,128)(2,1)S(1)} %get-tuple-element.540, bf16[2,512,12,64]{1,3,2,0:T(8,128)(2,1)S(1)} %get-tuple-element.538, s32[]{:T(128)S(6)} %copy.100), kind=kOutput, calls=%fused_computation.28.clone.1 | convolution fusion | flops 805306368 | bytes 27525124 | tf_op jit(solution)/shard_map/while/body/eval_jaxpr/while/body/eval_jaxpr/qhd,khd->hqk/dot_general | solution.py:28
  278.8 12.9 %bitcast_add_fusion.5 = f32[1024,12,64]{0,2,1:T(8,128)} fusion(f32[1024,12,64]{0,2,1:T(8,128)} %get-tuple-element.524, f32[12,512,1024]{2,1,0:T(8,128)} %fusion.112, f32[12,512]{1,0:T(8,128)S(1)} %dynamic-slice_bitcast_fusion.2, pred[1024]{0:T(1024)(128)(4,1)S(1)} %iota_compare_fusion.6, pred[]{:T(512)S(6)} %compare.3, ...), kind=kOutput, calls=%fused_computation.21.clone.1 | convolution fusion | flops 832045056 | bytes 32277508 | tf_op jit(solution)/shard_map/while/body/eval_jaxpr/while/body/eval_jaxpr/hqk,qhd->khd/dot_general | solution.py:70
  291.7 17.4 %multiply_reduce_fusion.7 = (f32[12,512]{1,0:T(8,128)S(1)}, f32[12,512,1024]{2,1,0:T(8,128)}) fusion(f32[12,512,1024]{2,1,0:T(8,128)} %fusion.112, f32[12,512]{1,0:T(8,128)S(1)} %dynamic-slice_bitcast_fusion.2, pred[1024]{0:T(1024)(128)(4,1)S(1)} %iota_compare_fusion.6, bf16[1024,12,64]{0,2,1:T(8,128)(2,1)} %get-tuple-element.543, ...), kind=kOutput, calls=%fused_computation.16.clone.1 | convolution fusion | flops 836757504 | bytes 52741124 | tf_op jit(solution)/shard_map/while/body/eval_jaxpr/while/body/eval_jaxpr/qhd,khd->hqk/dot_general | solution.py:60
  309.1 21.5 %multiply_convert_fusion.5 = bf16[12,512,1024]{2,1,0:T(8,128)(2,1)} fusion(f32[12,512,1024]{2,1,0:T(8,128)} %get-tuple-element.484, f32[12,512,1024]{2,1,0:T(8,128)} %fusion.112, f32[12,512]{1,0:T(8,128)S(1)} %get-tuple-element.485, f32[12,512]{1,0:T(8,128)S(1)} %dynamic-slice_bitcast_fusion.2, pred[1024]{0:T(1024)(128)(4,1)S(1)} %iota_compare_fusion.6), kind=kLoop, calls=%fused_computation.15.clone.1 | loop fusion | flops 37748736 | bytes 62964736 | tf_op jit(solution)/shard_map/while/body/eval_jaxpr/while/body/eval_jaxpr/convert_element_type | solution.py:62
  330.6 9.4 %bitcast_dynamic-update-slice_fusion.8 = bf16[2,512,12,64]{1,3,2,0:T(8,128)(2,1)} fusion(bf16[2,512,12,64]{1,3,2,0:T(8,128)(2,1)} %get-tuple-element.525, s32[]{:T(128)S(6)} %copy.100, bf16[12,512,1024]{2,1,0:T(8,128)(2,1)} %multiply_convert_fusion.5, bf16[1024,12,64]{0,2,1:T(8,128)(2,1)S(1)} %get-tuple-element.540), kind=kOutput, calls=%fused_computation.23.clone.1 | convolution fusion | flops 805699584 | bytes 15728644 | tf_op jit(solution)/shard_map/while/body/eval_jaxpr/while/body/eval_jaxpr/hqk,khd->qhd/dot_general | solution.py:64
  339.9 8.6 %bitcast_add_fusion.4 = f32[1024,12,64]{0,2,1:T(8,128)} fusion(f32[1024,12,64]{0,2,1:T(8,128)} %get-tuple-element.523, bf16[12,512,1024]{2,1,0:T(8,128)(2,1)} %multiply_convert_fusion.5, pred[]{:T(512)S(6)} %compare.3, bf16[2,512,12,64]{1,3,2,0:T(8,128)(2,1)S(1)} %get-tuple-element.538, s32[]{:T(128)S(6)} %copy.100), kind=kOutput, calls=%fused_computation.22.clone.1 | convolution fusion | flops 807665664 | bytes 19660804 | tf_op jit(solution)/shard_map/while/body/eval_jaxpr/while/body/eval_jaxpr/hqk,qhd->khd/dot_general | solution.py:68
  349.2 10.1 %fusion.112 = f32[12,512,1024]{2,1,0:T(8,128)} fusion(bf16[1024,12,64]{0,2,1:T(8,128)(2,1)S(1)} %get-tuple-element.540, bf16[2,512,12,64]{1,3,2,0:T(8,128)(2,1)S(1)} %get-tuple-element.538, s32[]{:T(128)S(6)} %copy.100), kind=kOutput, calls=%fused_computation.28.clone.1 | convolution fusion | flops 805306368 | bytes 27525124 | tf_op jit(solution)/shard_map/while/body/eval_jaxpr/while/body/eval_jaxpr/qhd,khd->hqk/dot_general | solution.py:28
  359.3 13.8 %bitcast_add_fusion.5 = f32[1024,12,64]{0,2,1:T(8,128)} fusion(f32[1024,12,64]{0,2,1:T(8,128)} %get-tuple-element.524, f32[12,512,1024]{2,1,0:T(8,128)} %fusion.112, f32[12,512]{1,0:T(8,128)S(1)} %dynamic-slice_bitcast_fusion.2, pred[1024]{0:T(1024)(128)(4,1)S(1)} %iota_compare_fusion.6, pred[]{:T(512)S(6)} %compare.3, ...), kind=kOutput, calls=%fused_computation.21.clone.1 | convolution fusion | flops 832045056 | bytes 32277508 | tf_op jit(solution)/shard_map/while/body/eval_jaxpr/while/body/eval_jaxpr/hqk,qhd->khd/dot_general | solution.py:70
  373.1 17.4 %multiply_reduce_fusion.7 = (f32[12,512]{1,0:T(8,128)S(1)}, f32[12,512,1024]{2,1,0:T(8,128)}) fusion(f32[12,512,1024]{2,1,0:T(8,128)} %fusion.112, f32[12,512]{1,0:T(8,128)S(1)} %dynamic-slice_bitcast_fusion.2, pred[1024]{0:T(1024)(128)(4,1)S(1)} %iota_compare_fusion.6, bf16[1024,12,64]{0,2,1:T(8,128)(2,1)} %get-tuple-element.543, ...), kind=kOutput, calls=%fused_computation.16.clone.1 | convolution fusion | flops 836757504 | bytes 52741124 | tf_op jit(solution)/shard_map/while/body/eval_jaxpr/while/body/eval_jaxpr/qhd,khd->hqk/dot_general | solution.py:60
  390.5 21.5 %multiply_convert_fusion.5 = bf16[12,512,1024]{2,1,0:T(8,128)(2,1)} fusion(f32[12,512,1024]{2,1,0:T(8,128)} %get-tuple-element.484, f32[12,512,1024]{2,1,0:T(8,128)} %fusion.112, f32[12,512]{1,0:T(8,128)S(1)} %get-tuple-element.485, f32[12,512]{1,0:T(8,128)S(1)} %dynamic-slice_bitcast_fusion.2, pred[1024]{0:T(1024)(128)(4,1)S(1)} %iota_compare_fusion.6), kind=kLoop, calls=%fused_computation.15.clone.1 | loop fusion | flops 37748736 | bytes 62964736 | tf_op jit(solution)/shard_map/while/body/eval_jaxpr/while/body/eval_jaxpr/convert_element_type | solution.py:62
  412.0 9.4 %bitcast_dynamic-update-slice_fusion.8 = bf16[2,512,12,64]{1,3,2,0:T(8,128)(2,1)} fusion(bf16[2,512,12,64]{1,3,2,0:T(8,128)(2,1)} %get-tuple-element.525, s32[]{:T(128)S(6)} %copy.100, bf16[12,512,1024]{2,1,0:T(8,128)(2,1)} %multiply_convert_fusion.5, bf16[1024,12,64]{0,2,1:T(8,128)(2,1)S(1)} %get-tuple-element.540), kind=kOutput, calls=%fused_computation.23.clone.1 | convolution fusion | flops 805699584 | bytes 15728644 | tf_op jit(solution)/shard_map/while/body/eval_jaxpr/while/body/eval_jaxpr/hqk,khd->qhd/dot_general | solution.py:64
  421.3 9.4 %bitcast_add_fusion.4 = f32[1024,12,64]{0,2,1:T(8,128)} fusion(f32[1024,12,64]{0,2,1:T(8,128)} %get-tuple-element.523, bf16[12,512,1024]{2,1,0:T(8,128)(2,1)} %multiply_convert_fusion.5, pred[]{:T(512)S(6)} %compare.3, bf16[2,512,12,64]{1,3,2,0:T(8,128)(2,1)S(1)} %get-tuple-element.538, s32[]{:T(128)S(6)} %copy.100), kind=kOutput, calls=%fused_computation.22.clone.1 | convolution fusion | flops 807665664 | bytes 19660804 | tf_op jit(solution)/shard_map/while/body/eval_jaxpr/while/body/eval_jaxpr/hqk,qhd->khd/dot_general | solution.py:68
  431.2 3.2 copy.75
  435.1 2.7 convert.29
  439.0 5.9 convolution_convert_fusion.2
  445.6 9.1 %convolution_convert_fusion = bf16[3072,768]{1,0:T(8,128)(2,1)} fusion(bf16[1024,3072]{1,0:T(8,128)(2,1)} %get-tuple-element.364, bf16[1024,768]{0,1:T(8,128)(2,1)} %copy.70, f32[1024]{0:T(1024)S(1)} %copy-done.32), kind=kOutput, calls=%fused_computation.46 | convolution fusion | flops 4836556800 | bytes 12587008 | tf_op jit(solution)/shard_map/dot_general | solution.py:154
  455.4 9.7 %convolution_convert_fusion.1 = bf16[768,3072]{1,0:T(8,128)(2,1)} fusion(bf16[1024,3072]{1,0:T(8,128)(2,1)} %copy-done.54, f32[1024,768]{0,1:T(8,128)} %copy-done.4, f32[768]{0:T(1024)S(1)} %copy-done.39, f32[768]{0:T(1024)S(1)} %copy-done.26, f32[1024]{0:T(1024)S(1)} %copy-done.30, f32[1024]{0:T(1024)S(1)} %copy-done.22), kind=kOutput, calls=%fused_computation.47 | convolution fusion | flops 4838129664 | bytes 14170112 | tf_op jit(solution)/shard_map/dot_general | solution.py:158
  468.4 4.3 all-gather.7
  472.8 19.9 %reduce-scatter.5.cloned.1.call-done = bf16[384,2304]{1,0:T(8,128)(2,1)} async-done(((bf16[768,2304]{1,0:T(8,128)(2,1)}), bf16[384,2304]{1,0:T(8,128)(2,1)}) %reduce-scatter.5.cloned.1.call-update) | async-done | bytes 1769488 | tf_op jit(solution)/shard_map/reduce_scatter | solution.py:198
  492.7 62.9 %reduce-scatter.11.cloned.1.call-done = bf16[1536,768]{1,0:T(8,128)(2,1)} async-done(((bf16[3072,768]{1,0:T(8,128)(2,1)}), bf16[1536,768]{1,0:T(8,128)(2,1)}) %reduce-scatter.11.cloned.1.call-update) | async-done | bytes 2359312 | tf_op jit(solution)/shard_map/reduce_scatter | solution.py:222
  555.6 63.0 %reduce-scatter.9.cloned.1.call-done = bf16[384,3072]{1,0:T(8,128)(2,1)} async-done(((bf16[768,3072]{1,0:T(8,128)(2,1)}), bf16[384,3072]{1,0:T(8,128)(2,1)}) %reduce-scatter.9.cloned.1.call-update) | async-done | bytes 2359312 | tf_op jit(solution)/shard_map/reduce_scatter | solution.py:216
  618.6 10.2 %multiply_convert_fusion.3 = bf16[1024,768]{0,1:T(8,128)(2,1)} fusion(f32[1024,768]{0,1:T(8,128)} %copy-done.4, bf16[1024,3072]{1,0:T(8,128)(2,1)} %get-tuple-element.364, bf16[3072,768]{1,0:T(8,128)(2,1)} %all-gather.19.cloned.1.call-done, f32[768]{0:T(1024)S(1)} %reshape.198, f32[1024]{0:T(1024)S(1)} %copy-done.32), kind=kOutput, calls=%fused_computation.73 | convolution fusion | flops 4834983936 | bytes 15735808 | tf_op jit(solution)/shard_map/dot_general | solution.py:149
  628.8 2.6 copy.79
  631.4 8.6 %fusion.61 = (bf16[768]{0:T(1024)(128)(2,1)S(1)}, f32[1024,768]{1,0:T(8,128)}) fusion(bf16[768,2304]{1,0:T(8,128)(2,1)} %all-gather.13.cloned.1.call-done, bf16[1024,768]{0,1:T(8,128)(2,1)} %bitcast.121, bf16[1024,768]{0,1:T(8,128)(2,1)} %bitcast.118, bf16[1024,768]{0,1:T(8,128)(2,1)S(1)} %bitcast.115), kind=kOutput, calls=%fused_computation.111 | convolution fusion | flops 3638820096 | bytes 11404800 | tf_op jit(solution)/shard_map/dot_general | solution.py:184
  640.0 3.5 copy.76
  643.5 2.5 fusion.55
  647.7 7.5 all-reduce.10
  655.8 61.8 %all-reduce.8 = (bf16[384]{0:T(512)(128)(2,1)S(1)}, bf16[384]{0:T(512)(128)(2,1)S(1)}, bf16[768]{0:T(1024)(128)(2,1)S(1)}, bf16[384]{0:T(512)(128)(2,1)S(1)}, bf...) all-reduce(bf16[384]{0:T(512)(128)(2,1)S(1)} %dynamic-slice.2, ...), channel_id=1, replica_groups=mesh['shard'=2,'rep'=16] {'rep'}, use_global_device_ids=true, to_apply=%region_17.18 | all-reduce | flops 4608 | bytes 18432 | tf_op jit(solution)/shard_map/psum | solution.py:230
  721.7 3.9 fusion.43
  727.7 47.0 %all-reduce.13.cloned.1.call-done = (bf16[384,2304]{1,0:T(8,128)(2,1)}, bf16[384,768]{1,0:T(8,128)(2,1)}, bf16[384,3072]{1,0:T(8,128)(2,1)}, bf16[1536,768]{1,0:T(8,128)(2,1)}) async-done(((bf16[384,2304]{1,0:T(8,128)(2,1)}, bf16[384,768]{1,0:T(8,128)(2,1)}, bf16[384,3072]{1,0:T(8,128)(2,1)}, bf16[1536,768]{1,0:T(8,128)(2,1)}), (bf16[384,2304]{1,0:T(8,128)(2,1)}, bf16[384,768]{1,0:T(8,128)(2,1)}, ...) | async-done | bytes 7077904 | tf_op jit(solution)/shard_map/psum | solution.py:232
  777.0 3.5 convert_element_type.207
  780.5 2.8 convert_element_type.218
  783.3 2.5 convert_element_type.221
  (221 shorter events, 49.4 us)
Async XLA Ops:
  7.2 3.6 copy-start.46
  7.2 8.9 %copy-start.47 = (bf16[384]{0:T(512)(128)(2,1)S(1)}, bf16[384]{0:T(512)(128)(2,1)}, u32[]{:S(2)}) copy-start(bf16[384]{0:T(512)(128)(2,1)} %param.23) | copy-start | bytes 2308
  7.2 13.3 %copy-start.48 = (bf16[384]{0:T(512)(128)(2,1)S(1)}, bf16[384]{0:T(512)(128)(2,1)}, u32[]{:S(2)}) copy-start(bf16[384]{0:T(512)(128)(2,1)} %param.27) | copy-start | bytes 2308
  7.2 18.3 %copy-start.49 = (bf16[384]{0:T(512)(128)(2,1)S(1)}, bf16[384]{0:T(512)(128)(2,1)}, u32[]{:S(2)}) copy-start(bf16[384]{0:T(512)(128)(2,1)} %param.28) | copy-start | bytes 2308
  7.2 23.2 %copy-start.50 = (bf16[384]{0:T(512)(128)(2,1)S(1)}, bf16[384]{0:T(512)(128)(2,1)}, u32[]{:S(2)}) copy-start(bf16[384]{0:T(512)(128)(2,1)} %param.29) | copy-start | bytes 2308
  7.2 54.8 %all-gather.13.cloned.1.call-start = ((), (), s32[]{:S(2)}) async-start(), calls=%async_computation.4 | async-start | bytes 5308416 | tf_op jit(solution)/shard_map/all_gather | solution.py:108
  8.0 27.4 %copy-start.44 = (bf16[768]{0:T(1024)(128)(2,1)S(1)}, bf16[768]{0:T(1024)(128)(2,1)}, u32[]{:S(2)}) copy-start(bf16[768]{0:T(1024)(128)(2,1)} %param.25) | copy-start | bytes 4612
  8.0 32.4 %copy-start.43 = (bf16[1536]{0:T(1024)(128)(2,1)S(1)}, bf16[1536]{0:T(1024)(128)(2,1)}, u32[]{:S(2)}) copy-start(bf16[1536]{0:T(1024)(128)(2,1)} %param.31) | copy-start | bytes 9220
  8.0 37.5 %copy-start.16 = (bf16[1024,768]{1,0:T(8,128)(2,1)S(1)}, bf16[1024,768]{1,0:T(8,128)(2,1)}, u32[]{:S(2)}) copy-start(bf16[1024,768]{1,0:T(8,128)(2,1)} %param.19) | copy-start | bytes 4718596
  8.0 149.7 %all-gather.15.cloned.1.call-start = ((), (), s32[]{:S(2)}) async-start(), calls=%async_computation.5 | async-start | bytes 1769472 | tf_op jit(solution)/shard_map/all_gather | solution.py:110
  8.7 155.6 %all-gather.17.cloned.1.call-start = ((), (), s32[]{:S(2)}) async-start(), calls=%async_computation.6 | async-start | bytes 7077888 | tf_op jit(solution)/shard_map/all_gather | solution.py:114
  9.5 205.2 %all-gather.19.cloned.1.call-start = ((), (), s32[]{:S(2)}) async-start(), calls=%async_computation.7 | async-start | bytes 7077888 | tf_op jit(solution)/shard_map/all_gather | solution.py:116
  10.1 462.7 %reduce-scatter.7.cloned.1.call-start = ((), (), s32[]{:S(2)}) async-start(), calls=%async_computation.9 | async-start | bytes 1769472 | tf_op jit(solution)/shard_map/reduce_scatter | solution.py:204
  16.1 45.9 %copy-start.23 = (f32[768]{0:T(1024)}, f32[768]{0:T(1024)S(1)}, u32[]{:S(2)}) copy-start(f32[768]{0:T(1024)S(1)} %reshape.191) | copy-start | bytes 9220
  20.5 41.5 %copy-start.40 = (f32[768]{0:T(1024)}, f32[768]{0:T(1024)S(1)}, u32[]{:S(2)}) copy-start(f32[768]{0:T(1024)S(1)} %reshape.192) | copy-start | bytes 9220
  46.3 15.7 %copy-start.2 = (bf16[1024,768]{0,1:T(8,128)(2,1)}, bf16[1024,768]{0,1:T(8,128)(2,1)S(1)}, u32[]{:S(2)}) copy-start(bf16[1024,768]{0,1:T(8,128)(2,1)S(1)} %copy.63) | copy-start | bytes 4718596
  46.3 2.0 copy-start.17
  46.5 21.9 %copy-start.19 = (f32[1024]{0:T(1024)}, f32[1024]{0:T(1024)S(1)}, u32[]{:S(2)}) copy-start(f32[1024]{0:T(1024)S(1)} %broadcast_multiply_fusion.5) | copy-start | bytes 12292
  48.2 20.2 %copy-start.27 = (f32[1024]{0:T(1024)}, f32[1024]{0:T(1024)S(1)}, u32[]{:S(2)}) copy-start(f32[1024]{0:T(1024)S(1)} %add_rsqrt_fusion.1) | copy-start | bytes 12292
  92.6 13.4 %copy-start.1 = (bf16[1024,12,64]{0,2,1:T(8,128)(2,1)S(1)}, bf16[1024,12,64]{0,2,1:T(8,128)(2,1)}, u32[]{:S(2)}) copy-start(bf16[1024,12,64]{0,2,1:T(8,128)(2,1)} %get-tuple-element.508) | copy-start | bytes 4718596 | tf_op jit(solution)/shard_map/while/body/eval_jaxpr/while
  92.6 13.5 %copy-start.12 = (bf16[2,512,12,64]{1,3,2,0:T(8,128)(2,1)S(1)}, bf16[2,512,12,64]{1,3,2,0:T(8,128)(2,1)}, u32[]{:S(2)}) copy-start(bf16[2,512,12,64]{1,3,2,0:T(8,128)(2,1)} %get-tuple-element.495) | copy-start | bytes 4718596 | tf_op jit(solution)/shard_map/while/body/eval_jaxpr/while
  117.3 1.1 copy-start.13
  129.2 11.4 %copy-start.1 = (bf16[1024,12,64]{0,2,1:T(8,128)(2,1)S(1)}, bf16[1024,12,64]{0,2,1:T(8,128)(2,1)}, u32[]{:S(2)}) copy-start(bf16[1024,12,64]{0,2,1:T(8,128)(2,1)} %get-tuple-element.508) | copy-start | bytes 4718596 | tf_op jit(solution)/shard_map/while/body/eval_jaxpr/while
  129.2 11.4 %copy-start.12 = (bf16[2,512,12,64]{1,3,2,0:T(8,128)(2,1)S(1)}, bf16[2,512,12,64]{1,3,2,0:T(8,128)(2,1)}, u32[]{:S(2)}) copy-start(bf16[2,512,12,64]{1,3,2,0:T(8,128)(2,1)} %get-tuple-element.495) | copy-start | bytes 4718596 | tf_op jit(solution)/shard_map/while/body/eval_jaxpr/while
  151.8 1.1 copy-start.13
  153.1 4.6 copy-start.42
  162.2 1.7 copy-start.4
  162.2 2.1 copy-start.25
  162.3 2.1 copy-start.33
  162.3 2.1 copy-start.38
  162.3 81.7 %copy-start.21 = (f32[1024]{0:T(1024)}, f32[1024]{0:T(1024)S(1)}, u32[]{:S(2)}) copy-start(f32[1024]{0:T(1024)S(1)} %broadcast_multiply_fusion.4) | copy-start | bytes 12292
  164.3 79.7 %copy-start.29 = (f32[1024]{0:T(1024)}, f32[1024]{0:T(1024)S(1)}, u32[]{:S(2)}) copy-start(f32[1024]{0:T(1024)S(1)} %add_rsqrt_fusion) | copy-start | bytes 12292
  164.4 50.3 %copy-start.31 = (f32[1024]{0:T(1024)S(1)}, f32[1024]{0:T(1024)}, u32[]{:S(2)}) copy-start(f32[1024]{0:T(1024)} %fusion.50) | copy-start | bytes 12292
  214.7 13.9 %copy-start.52 = (bf16[768,3072]{1,0:T(8,128)(2,1)S(1)}, bf16[768,3072]{1,0:T(8,128)(2,1)}, u32[]{:S(2)}) copy-start(bf16[768,3072]{1,0:T(8,128)(2,1)} %all-gather.17.cloned.1.call-done) | copy-start | bytes 14155780
  228.6 7.3 copy-start.54
  239.4 4.6 copy-start.5
  239.4 4.7 copy-start.7
  244.1 5.6 copy-start.18
  248.0 1.7 copy-start.9
  252.2 240.5 %reduce-scatter.5.cloned.1.call-start = ((), (), s32[]{:S(2)}) async-start(), calls=%async_computation.8 | async-start | bytes 5308416 | tf_op jit(solution)/shard_map/reduce_scatter | solution.py:198
  268.6 10.2 %copy-start.8 = (bf16[2,512,12,64]{1,3,2,0:T(8,128)(2,1)S(1)}, bf16[2,512,12,64]{1,3,2,0:T(8,128)(2,1)}, u32[]{:S(2)}) copy-start(bf16[2,512,12,64]{1,3,2,0:T(8,128)(2,1)} %get-tuple-element.542) | copy-start | bytes 4718596 | tf_op jit(solution)/shard_map/while/body/eval_jaxpr/while
  349.2 10.1 %copy-start.8 = (bf16[2,512,12,64]{1,3,2,0:T(8,128)(2,1)S(1)}, bf16[2,512,12,64]{1,3,2,0:T(8,128)(2,1)}, u32[]{:S(2)}) copy-start(bf16[2,512,12,64]{1,3,2,0:T(8,128)(2,1)} %get-tuple-element.542) | copy-start | bytes 4718596 | tf_op jit(solution)/shard_map/while/body/eval_jaxpr/while
  431.2 3.6 copy-start
  435.0 2.8 copy-start.10
  435.0 3.9 copy-start.3
  435.1 3.9 copy-start.20
  435.1 3.9 copy-start.24
  435.1 3.9 copy-start.28
  435.1 3.9 copy-start.41
  437.8 1.2 copy-start.11
  444.9 110.7 %reduce-scatter.11.cloned.1.call-start = ((), (), s32[]{:S(2)}) async-start(), calls=%async_computation.11 | async-start | bytes 7077888 | tf_op jit(solution)/shard_map/reduce_scatter | solution.py:222
  454.7 0.7 copy-start.30
  454.7 0.7 copy-start.39
  454.8 163.8 %reduce-scatter.9.cloned.1.call-start = ((), (), s32[]{:S(2)}) async-start(), calls=%async_computation.10 | async-start | bytes 7077888 | tf_op jit(solution)/shard_map/reduce_scatter | solution.py:216
  465.2 3.2 copy-start.51
  465.2 309.5 %all-reduce.13.cloned.1.call-start = ((), (), s32[]{:S(2)}) async-start(), calls=%async_computation.12 | async-start | bytes 14155776 | tf_op jit(solution)/shard_map/psum | solution.py:232
  643.5 3.0 copy-start.6
  646.0 1.6 copy-start.34
  646.0 1.6 copy-start.35
  646.0 1.6 copy-start.36
  646.1 1.6 copy-start.37
  646.1 1.6 copy-start.45
  774.7 5.8 copy-start.15
  780.5 2.8 copy-start.14
  (4 other events, 2.7 us)
Sparse Core Ops, SparseCore 0:
  9.6 52.3 all-gather.12
  63.5 22.7 all-gather.14
  87.9 62.6 all-gather.16
  152.0 62.6 all-gather.18
  252.3 21.7 reduce-scatter.6
  445.1 47.6 reduce-scatter.4
  495.6 59.9 reduce-scatter.10
  558.6 59.9 reduce-scatter.8
  622.7 152.0 all-reduce.12
where the time goes:
time: 802 us; the launch traced here: 793 us
  matrix products  259 us (32%)
  waiting for transfers between devices  243 us (30%)
  other arithmetic  107 us (13%)
  blocking collectives  105 us (13%)
  local copies, waits for them, and re-layouts  59.5 us (7%)
  between operations  17.3 us (2%)
    reduce_scatter x1, waiting for transfers between devices, shards(): lax.psum_scatter(expand_weight_slope.astype(jnp.bfloat16), 'shard', scatt...  63 us
    reduce_scatter x1, waiting for transfers between devices, shards(): lax.psum_scatter(reduce_weight_slope.astype(jnp.bfloat16), 'shard', scatt...  62.9 us
    psum x1, blocking collectives, shards(): lax.psum(owned[0].astype(jnp.bfloat16), 'rep').astype(jnp.float32)  61.8 us
    psum x1, waiting for transfers between devices, shards(): lax.psum(owned[2].astype(jnp.bfloat16), 'rep').astype(jnp.float32)  47 us
    convert_element_type x2, other arithmetic, one_block(): dscores = (probs * (dprobs - delta)).astype(jnp.bfloat16)  42.9 us
    dot_general x4, matrix products, block_scores(): jnp.einsum('qhd,khd->hqk', piece, keys, preferred_element_type=jnp.float32)  40.5 us
    all_gather x1, waiting for transfers between devices, shards(): lax.all_gather(reduce_weight, 'shard', axis=0, tiled=True)  35.8 us
    dot_general x2, matrix products, one_block(): jnp.einsum('qhd,khd->hqk', block_grad, values, preferred_element_type=jnp...  34.8 us
  transfers between devices with their start and end apart: 9, of which 6 were waited for; matrix products, arithmetic and copies ran while one was open for 46% of the time, Pallas kernels for 0%

commit v1 on v0

v1 whole, which is shorter than its diff:
```python
import functools

import jax
import jax.numpy as jnp
from jax import lax
from jax.experimental import pallas as pl
from jax.experimental.pallas import tpu as pltpu
from jax.sharding import PartitionSpec as P

D = 768
H = 12
SEQ = 1024
FF = 3072
bf = jnp.bfloat16
f32 = jnp.float32
NN = (((1,), (0,)), ((), ()))
NT = (((1,), (1,)), ((), ()))
TN = (((0,), (0,)), ((), ()))
VM = pl.BlockSpec(memory_space=pltpu.VMEM)
SM = pl.BlockSpec(memory_space=pltpu.SMEM)
HB = pl.BlockSpec(memory_space=pl.ANY)
VLIMIT = 60 * 2**20
RB = 256


def dot(a, b, dims=NN):
    return lax.dot_general(a, b, dims, preferred_element_type=f32)


def lanes(shape):
    return lax.broadcasted_iota(jnp.int32, shape, 1)


def rowsi(shape):
    return lax.broadcasted_iota(jnp.int32, shape, 0)


def norm(v):
    mean = jnp.mean(v, axis=-1, keepdims=True)
    c = v - mean
    r = lax.rsqrt(jnp.mean(c * c, axis=-1, keepdims=True) + 1e-05)
    return c * r, r


def norm_back(up, n, r, gain):
    e = up * gain
    return r * (e - jnp.mean(e, axis=-1, keepdims=True) - n * jnp.mean(e * n, axis=-1, keepdims=True))


def three(v):
    hi = v.astype(bf).astype(f32)
    mid = (v - hi).astype(bf).astype(f32)
    return hi, mid, v - hi - mid


def fwd_pair(hp, length, qkv_ref, o_ref, lse_ref):
    QB = 512
    cq = pl.multiple_of(hp * 128, 128)
    q = qkv_ref[:, pl.ds(cq, 128)]
    k = qkv_ref[:, pl.ds(pl.multiple_of(cq + D, 128), 128)]
    v = qkv_ref[:, pl.ds(pl.multiple_of(cq + 2 * D, 128), 128)]
    vt = v.T
    ln = lanes((SEQ, 128))
    rw = rowsi((SEQ, 128))
    kaug = jnp.where((ln == 0) & (rw >= length), -1e30, 0.0).astype(bf)
    qaug = (lanes((QB, 128)) == 0).astype(f32).astype(bf)
    vr = rowsi((128, SEQ))
    ksides = []
    vts = []
    for h in range(2):
        half = (ln < 64) if h == 0 else (ln >= 64)
        ksides.append(jnp.concatenate([jnp.where(half, k, jnp.zeros_like(k)), kaug], axis=1))
        vh = (vr < 64) if h == 0 else (vr >= 64)
        vts.append(jnp.where(vh, vt, jnp.ones_like(vt)))
    items = [(qb, h) for qb in range(SEQ // QB) for h in range(2)]

    def scores(it):
        qb, h = it
        qs = jnp.concatenate([q[qb * QB : (qb + 1) * QB], qaug], axis=1)
        return dot(ksides[h], qs, NT)

    res = {}
    s_next = scores(items[0])
    for i, it in enumerate(items):
        s = s_next
        if i + 1 < len(items):
            s_next = scores(items[i + 1])
        m = jnp.max(s, axis=0, keepdims=True)
        p = jnp.exp(s - m).astype(bf)
        ot = dot(vts[it[1]], p)
        qb, h = it
        total = ot[64:65] if h == 0 else ot[0:1]
        res[it] = ot / total
        lse_ref[pl.ds(2 * hp + h, 1), qb * QB : (qb + 1) * QB] = m + jnp.log(total)
        if h == 1:
            op = jnp.where(rowsi((128, QB)) < 64, res[(qb, 0)], res[(qb, 1)])
            o_ref[qb * QB : (qb + 1) * QB, pl.ds(cq, 128)] = op.astype(bf).T


def bwd_pair(hp, length, qkv_ref, do_ref, augq_ref, augd_ref, dqkv_ref):
    KB = 512
    cq = pl.multiple_of(hp * 128, 128)
    ck = pl.multiple_of(cq + D, 128)
    cv = pl.multiple_of(cq + 2 * D, 128)
    q = qkv_ref[:, pl.ds(cq, 128)]
    k = qkv_ref[:, pl.ds(ck, 128)]
    v = qkv_ref[:, pl.ds(cv, 128)]
    do = do_ref[:, pl.ds(cq, 128)]
    qt = q.T
    dot_ = do.T
    qs = jnp.concatenate([q, augq_ref[...]], axis=1)
    ds_ = jnp.concatenate([do, augd_ref[...]], axis=1)
    lb = lanes((KB, 128))
    rb = rowsi((KB, 128))

    def first(it):
        kb, h = it
        half = (lb < 64) if h == 0 else (lb >= 64)
        hh = 2 * hp + h
        neg = jnp.where((lb == hh) | (lb == hh + 16) | (lb == hh + 32), -1.0, 0.0)
        aug = jnp.where((lb == 48) & (rb + kb * KB >= length), -1e30, neg).astype(bf)
        kk = k[kb * KB : (kb + 1) * KB]
        vv = v[kb * KB : (kb + 1) * KB]
        z = jnp.zeros_like(kk)
        ks = jnp.concatenate([jnp.where(half, kk, z), aug], axis=1)
        vs = jnp.concatenate([jnp.where(half, vv, z), aug], axis=1)
        return dot(qs, ks, NT), dot(ds_, vs, NT), kk

    items = [(kb, h) for kb in range(SEQ // KB) for h in range(2)]
    dq = [None, None]
    dk = {}
    dv = {}
    nxt = first(items[0])
    for i, it in enumerate(items):
        s, dp, kk = nxt
        if i + 1 < len(items):
            nxt = first(items[i + 1])
        kb, h = it
        p = jnp.exp(s)
        pb = p.astype(bf)
        dsb = (p * dp).astype(bf)
        rs = slice(0, 64) if h == 0 else slice(64, 128)
        dv[it] = dot(dot_[rs], pb)
        dk[it] = dot(qt[rs], dsb)
        t = dot(dsb, kk)
        dq[h] = t if dq[h] is None else dq[h] + t
        if h == 1:
            dkp = jnp.concatenate([dk[(kb, 0)], dk[(kb, 1)]], axis=0).astype(bf)
            dvp = jnp.concatenate([dv[(kb, 0)], dv[(kb, 1)]], axis=0).astype(bf)
            dqkv_ref[kb * KB : (kb + 1) * KB, pl.ds(ck, 128)] = dkp.T
            dqkv_ref[kb * KB : (kb + 1) * KB, pl.ds(cv, 128)] = dvp.T
    dqkv_ref[:, pl.ds(cq, 128)] = (jnp.where(lanes((SEQ, 128)) < 64, dq[0], dq[1]) * 0.125).astype(bf)


def front_kernel(len_ref, x_ref, g_ref, b_ref, wa_ref, ba_ref, h_ref, qkv_ref, o_ref, aug_ref, lse_ref):
    length = len_ref[0]

    def rows(i, _):
        r = pl.ds(pl.multiple_of(i * RB, RB), RB)
        n, _r = norm(x_ref[r, :].astype(f32))
        h_ref[r, :] = (n * g_ref[...] + b_ref[...]).astype(bf)
        return 0

    lax.fori_loop(0, SEQ // RB, rows, 0)

    def cols(j, _):
        c = pl.ds(pl.multiple_of(j * 256, 256), 256)
        t = dot(h_ref[...], wa_ref[:, c]) + ba_ref[:, c]
        t = t.astype(bf).astype(f32) * jnp.where(j < D // 256, 0.125, 1.0)
        qkv_ref[:, c] = t.astype(bf)
        return 0

    lax.fori_loop(0, 3 * D // 256, cols, 0)
    lse_ref[...] = jnp.zeros_like(lse_ref)

    def pair(hp, _):
        fwd_pair(hp, length, qkv_ref, o_ref, lse_ref)
        return 0

    lax.fori_loop(0, H // 2, pair, 0)
    hi, mid, lo = three(lse_ref[...])
    one = jnp.where(rowsi((80, SEQ)) == 0, 1.0, 0.0)
    aug_ref[...] = jnp.concatenate([hi, mid, lo, one], axis=0).astype(bf).T


def front(length, x, g1, b1, wa, ba):
    return pl.pallas_call(
        front_kernel,
        out_shape=(
            jax.ShapeDtypeStruct((SEQ, D), bf),
            jax.ShapeDtypeStruct((SEQ, 3 * D), bf),
            jax.ShapeDtypeStruct((SEQ, D), bf),
            jax.ShapeDtypeStruct((SEQ, 128), bf),
        ),
        in_specs=[SM] + [VM] * 5,
        out_specs=(VM,) * 4,
        scratch_shapes=[pltpu.VMEM((16, SEQ), f32)],
        compiler_params=pltpu.CompilerParams(vmem_limit_bytes=VLIMIT),
        cost_estimate=pl.CostEstimate(flops=7 * 10**9, bytes_accessed=10**7, transcendentals=12 * 2**20),
        name="front",
    )(length, x, g1, b1, wa, ba)


def mid_kernel(
    W, len_ref, x_ref, o_ref, cot_ref, wo_ref, bo_ref, g_ref, b_ref, w1_any, be_ref, w2_any, br_ref,
    out_ref, dx_ref, do_ref, augd_ref, dw1_ref, dw2_ref, dwo_ref, dbe_ref, dsm_ref,
    w1_ref, w2_ref, x1_ref, y_ref, dh_ref, h_ref, gb_ref, dxb_ref, sem,
):
    length = len_ref[0]
    c1 = pltpu.make_async_copy(w1_any, w1_ref, sem.at[0])
    c2 = pltpu.make_async_copy(w2_any, w2_ref, sem.at[1])
    c1.start()
    c2.start()

    def rows(i, acc):
        r = pl.ds(pl.multiple_of(i * RB, RB), RB)
        x1 = x_ref[r, :].astype(f32) + (dot(o_ref[r, :], wo_ref[...]) + bo_ref[...])
        x1_ref[r, :] = x1
        n, _r = norm(x1)
        h_ref[r, :] = (n * g_ref[...] + b_ref[...]).astype(bf)
        live = (rowsi((RB, 1)) + i * RB) < length
        gb = jnp.where(live, cot_ref[r, :].astype(f32), 0.0)
        gb_ref[r, :] = gb.astype(bf)
        y_ref[r, :] = jnp.zeros((RB, D), f32)
        dh_ref[r, :] = jnp.zeros((RB, D), f32)
        return acc + jnp.sum(gb, axis=0, keepdims=True)

    dsm_ref[0:1, :] = lax.fori_loop(0, SEQ // RB, rows, jnp.zeros((1, D), f32))
    c1.wait()
    c2.wait()

    def chunk(j, _):
        lo = pl.multiple_of(j * W, W)
        parts = [pl.ds(pl.multiple_of(lo + s * (FF // 2), W), W) for s in range(2)]
        for s, c in enumerate(parts):
            w1 = w1_ref[:, c]
            w2 = w2_ref[c, :]
            u = dot(h_ref[...], w1) + be_ref[:, c]
            sig = 0.5 * jnp.tanh(0.851 * u) + 0.5
            a = u * sig
            ab = a.astype(bf)
            y_ref[...] += dot(ab, w2)
            dw2_ref[c, :] = dot(ab, gb_ref[...], TN).astype(bf)
            da = dot(gb_ref[...], w2, NT)
            du = da * (sig * (1.0 + 1.702 * (u - a)))
            dub = du.astype(bf)
            dbe_ref[:, c] = jnp.sum(du, axis=0, keepdims=True)
            dw1_ref[:, c] = dot(h_ref[...], dub, TN).astype(bf)
            dh_ref[...] += dot(dub, w1, NT)
        return 0

    lax.fori_loop(0, FF // (2 * W), chunk, 0)
    hl = lanes((D, 128)) % 16
    sel = jnp.where((hl == rowsi((D, 128)) // 64) & (lanes((D, 128)) < 48), 1.0, 0.0).astype(bf)

    def last(i, acc):
        r = pl.ds(pl.multiple_of(i * RB, RB), RB)
        x1 = x1_ref[r, :]
        live = (rowsi((RB, 1)) + i * RB) < length
        out_ref[r, :] = jnp.where(live, x1 + (y_ref[r, :] + br_ref[...]), 0.0).astype(bf)
        n, rs = norm(x1)
        dh = dh_ref[r, :]
        dx = gb_ref[r, :].astype(f32) + norm_back(dh, n, rs, g_ref[...])
        dx_ref[r, :] = dx
        dxb = dx.astype(bf)
        dxb_ref[r, :] = dxb
        do = dot(dxb, wo_ref[...], NT).astype(bf)
        do_ref[r, :] = do
        prod = do.astype(f32) * o_ref[r, :].astype(f32)
        phi = prod.astype(bf)
        dl = dot(phi, sel) + dot((prod - phi.astype(f32)).astype(bf), sel)
        hi, mid, lo = three(dl)
        ln = lanes((RB, 128))
        augd_ref[r, :] = jnp.where(ln < 16, hi, jnp.where(ln < 32, mid, lo)).astype(bf)
        return (
            acc[0] + jnp.sum(dh * n, axis=0, keepdims=True),
            acc[1] + jnp.sum(dh, axis=0, keepdims=True),
            acc[2] + jnp.sum(dx, axis=0, keepdims=True),
        )

    z = jnp.zeros((1, D), f32)
    a0, a1, a2 = lax.fori_loop(0, SEQ // RB, last, (z, z, z))
    dsm_ref[1:2, :] = a0
    dsm_ref[2:3, :] = a1
    dsm_ref[3:4, :] = a2
    dwo_ref[...] = dot(o_ref[...], dxb_ref[...], TN).astype(bf)


def middle(length, x, o, cot, wo, bo, g2, b2, w1, be, w2, br):
    return pl.pallas_call(
        functools.partial(mid_kernel, 256),
        out_shape=(
            jax.ShapeDtypeStruct((SEQ, D), bf),
            jax.ShapeDtypeStruct((SEQ, D), f32),
            jax.ShapeDtypeStruct((SEQ, D), bf),
            jax.ShapeDtypeStruct((SEQ, 128), bf),
            jax.ShapeDtypeStruct((D, FF), bf),
            jax.ShapeDtypeStruct((FF, D), bf),
            jax.ShapeDtypeStruct((D, D), bf),
            jax.ShapeDtypeStruct((1, FF), f32),
            jax.ShapeDtypeStruct((4, D), f32),
        ),
        in_specs=[SM] + [VM] * 7 + [HB, VM, HB, VM],
        out_specs=(VM,) * 9,
        scratch_shapes=[
            pltpu.VMEM((D, FF), bf),
            pltpu.VMEM((FF, D), bf),
            pltpu.VMEM((SEQ, D), f32),
            pltpu.VMEM((SEQ, D), f32),
            pltpu.VMEM((SEQ, D), f32),
            pltpu.VMEM((SEQ, D), bf),
            pltpu.VMEM((SEQ, D), bf),
            pltpu.VMEM((SEQ, D), bf),
            pltpu.SemaphoreType.DMA((2,)),
        ],
        compiler_params=pltpu.CompilerParams(vmem_limit_bytes=VLIMIT),
        cost_estimate=pl.CostEstimate(flops=33 * 10**9, bytes_accessed=3 * 10**7, transcendentals=3 * 2**20),
        name="middle",
    )(length, x, o, cot, wo, bo, g2, b2, w1, be, w2, br)


def back_kernel(len_ref, qkv_ref, do_ref, augq_ref, augd_ref, h_ref, x_ref, dx_ref, g_ref, wa_ref,
                ts_ref, dwa_ref, dba_ref, dsm_ref, dqkv_ref, dh_ref):
    length = len_ref[0]

    def pair(hp, _):
        bwd_pair(hp, length, qkv_ref, do_ref, augq_ref, augd_ref, dqkv_ref)
        return 0

    lax.fori_loop(0, H // 2, pair, 0)

    def cols(j, _):
        c = pl.ds(pl.multiple_of(j * 256, 256), 256)
        d = dqkv_ref[:, c]
        dba_ref[:, c] = jnp.sum(d.astype(f32), axis=0, keepdims=True)
        dwa_ref[:, c] = dot(h_ref[...], d, TN).astype(bf)
        return 0

    lax.fori_loop(0, 3 * D // 256, cols, 0)

    def rows(i, acc):
        r = pl.ds(pl.multiple_of(i * RB, RB), RB)
        dh = dot(dqkv_ref[r, :], wa_ref[...], NT)
        n, rs = norm(x_ref[r, :].astype(f32))
        ts_ref[r, :] = (dx_ref[r, :] + norm_back(dh, n, rs, g_ref[...])).astype(bf)
        return acc[0] + jnp.sum(dh * n, axis=0, keepdims=True), acc[1] + jnp.sum(dh, axis=0, keepdims=True)

    z = jnp.zeros((1, D), f32)
    a0, a1 = lax.fori_loop(0, SEQ // RB, rows, (z, z))
    dsm_ref[0:1, :] = a0
    dsm_ref[1:2, :] = a1


def back(length, qkv, do, augq, augd, h1, x, dx, g1, wa):
    return pl.pallas_call(
        back_kernel,
        out_shape=(
            jax.ShapeDtypeStruct((SEQ, D), bf),
            jax.ShapeDtypeStruct((D, 3 * D), bf),
            jax.ShapeDtypeStruct((1, 3 * D), f32),
            jax.ShapeDtypeStruct((2, D), f32),
        ),
        in_specs=[SM] + [VM] * 9,
        out_specs=(VM,) * 4,
        scratch_shapes=[pltpu.VMEM((SEQ, 3 * D), bf), pltpu.VMEM((SEQ, D), f32)],
        compiler_params=pltpu.CompilerParams(vmem_limit_bytes=VLIMIT),
        cost_estimate=pl.CostEstimate(flops=16 * 10**9, bytes_accessed=2 * 10**7, transcendentals=12 * 2**20),
        name="back",
    )(length, qkv, do, augq, augd, h1, x, dx, g1, wa)


def shards(x, lengths, cot, g1, b1, wa, ba, wo, bo, g2, b2, w1, be, w2, br):
    def gather(v):
        return lax.all_gather(v, "shard", axis=0, tiled=True)

    smalls = [g1, b1, ba, bo, g2, b2, be, br]
    packed = lax.all_gather(jnp.concatenate(smalls), "shard", axis=0)
    full = []
    at = 0
    for v in smalls:
        full.append(packed[:, at : at + v.shape[0]].reshape(1, -1).astype(f32))
        at += v.shape[0]
    g1, b1, ba, bo, g2, b2, be, br = full
    ba = jnp.concatenate([ba[:, :D], jnp.zeros((1, D), f32), ba[:, D:]], axis=1)
    wa, wo, w1, w2 = gather(wa), gather(wo), gather(w1), gather(w2)
    h1, qkv, o, augq = front(lengths, x, g1, b1, wa, ba)
    out, dx, do, augd, dw1, dw2, dwo, dbe, sm = middle(lengths, x, o, cot, wo, bo, g2, b2, w1, be, w2, br)
    ts, dwa, dba, sm1 = back(lengths, qkv, do, augq, augd, h1, x, dx, g1, wa)

    def reduce_big(v):
        v = lax.psum_scatter(v, "shard", scatter_dimension=0, tiled=True)
        return lax.psum(v, "rep").astype(f32)

    n = lax.axis_size("shard")
    me = lax.axis_index("shard")
    parts = [sm1[0], sm1[1], dba[0, :D], dba[0, 2 * D :], sm[3], sm[1], sm[2], dbe[0], sm[0]]
    total = lax.psum(jnp.concatenate(parts), ("shard", "rep"))
    got = []
    at = 0
    for v in parts:
        got.append(total[at : at + v.shape[0]])
        at += v.shape[0]
    dg1, db1, dbq, dbv, dbo, dg2, db2, dbe, dbr = got
    dba = jnp.concatenate([dbq, dbv])

    def own(v):
        w = v.shape[0] // n
        return lax.dynamic_slice(v, (me * w,), (w,))

    return (
        out, ts, own(dg1), own(db1), reduce_big(dwa), own(dba), reduce_big(dwo), own(dbo), own(dg2), own(db2),
        reduce_big(dw1), own(dbe), reduce_big(dw2), own(dbr),
    )


def solution(mesh):
    rows = P(("shard", "rep"), None)
    vec = P("shard")
    mat = P("shard", None)
    in_specs = (rows, P(("shard", "rep")), rows, vec, vec, mat, vec, mat, vec, vec, vec, mat, vec, mat, vec)
    out_specs = (rows, rows, vec, vec, mat, vec, mat, vec, vec, vec, mat, vec, mat, vec)
    return jax.shard_map(shards, mesh=mesh, in_specs=in_specs, out_specs=out_specs, check_vma=False)
```

time: 802 us -> 672 us (0.84); the launches traced: 793 us -> 671 us
  matrix products: 259 us -> 0 us
  waiting for transfers between devices: 243 us -> 447 us
  Pallas kernels: 0 us -> 140 us
  other arithmetic: 107 us -> 10.9 us
  blocking collectives: 105 us -> 47 us
  local copies, waits for them, and re-layouts: 59.5 us -> 12.1 us
    dot_general x26 -> x0, matrix products: 259 us -> none  [the longest x4 40.5 us: block_scores(): jnp.einsum('qhd,khd->hqk', piece, keys, preferred_element_type=jnp.float32)]
    pallas_call x0 -> x3, Pallas kernels: none -> 140 us  [the longest x1 61.7 us: middle(): pl.pallas_call(functools.partial(mid_kernel, 256), out_shape=(jax.ShapeDt...]
    all_gather x4, waiting for transfers between devices: 47.9 us -> 162 us  [gather(): return lax.all_gather(v, 'shard', axis=0, tiled=True)]
    psum x1, waiting for transfers between devices: 47 us -> 109 us  [reduce_big(): return lax.psum(v, 'rep').astype(f32)]
    convert_element_type x24 -> x4, other arithmetic: 63.9 us -> 10.2 us  [reduce_big(): return lax.psum(v, 'rep').astype(f32)]
    reduce_sum x9 -> x0, other arithmetic: 38 us -> none  [the longest x2 24.8 us: one_block(): total = jnp.sum(expo, axis=-1, keepdims=True)]
    all_gather x8 -> x1, blocking collectives: 35.7 us -> 5.54 us  [shards(): packed = lax.all_gather(jnp.concatenate(smalls), 'shard', axis=0)]
    reduce_scatter x4, waiting for transfers between devices: 146 us -> 172 us  [reduce_big(): v = lax.psum_scatter(v, 'shard', scatter_dimension=0, tiled=True)]
  transfers between devices with their start and end apart: 9 -> 9, of which waited for: 6 -> 7; matrix products, arithmetic and copies ran while one was open for 46% -> 2% of each run, Pallas kernels for 0% -> 12%
where the time goes in v1:
time: 672 us; the launch traced here: 671 us
  waiting for transfers between devices  447 us (67%)
  Pallas kernels  140 us (21%)
  blocking collectives  47 us (7%)
  between operations  14.8 us (2%)
  local copies, waits for them, and re-layouts  12.1 us (2%)
  other arithmetic  10.9 us (2%)
    reduce_scatter x4, waiting for transfers between devices, reduce_big(): v = lax.psum_scatter(v, 'shard', scatter_dimension=0, tiled=True)  172 us
    all_gather x4, waiting for transfers between devices, gather(): return lax.all_gather(v, 'shard', axis=0, tiled=True)  162 us
    psum x1, waiting for transfers between devices, reduce_big(): return lax.psum(v, 'rep').astype(f32)  109 us
    pallas_call x1, Pallas kernels, middle(): pl.pallas_call(functools.partial(mid_kernel, 256), out_shape=(jax.ShapeDt...  61.7 us
    pallas_call x1, Pallas kernels, back(): pl.pallas_call(back_kernel, out_shape=(jax.ShapeDtypeStruct((SEQ, D), bf)...  48.6 us
    psum x1, blocking collectives, shards(): total = lax.psum(jnp.concatenate(parts), ('shard', 'rep'))  41.4 us
    pallas_call x1, Pallas kernels, front(): pl.pallas_call(front_kernel, out_shape=(jax.ShapeDtypeStruct((SEQ, D), bf...  29.3 us
  transfers between devices with their start and end apart: 9, of which 7 were waited for; matrix products, arithmetic and copies ran while one was open for 2% of the time, Pallas kernels for 12%

profile of v1, /device:TPU:0, one launch (start us, length us, event | category | flops | bytes accessed | tf_op | source)
XLA Modules:
  0.0 671.3 jit_solution(9495090722607801333)
XLA Ops:
  7.2 0.0 all-gather.7.cloned.1.call-start
  7.2 0.7 all-gather.7.cloned.1.call-update
  7.9 0.0 all-gather.9.cloned.1.call-start
  8.0 0.7 all-gather.9.cloned.1.call-update
  8.7 0.0 copy-start.9
  8.7 0.0 all-gather.11.cloned.1.call-start
  8.8 0.7 all-gather.11.cloned.1.call-update
  9.5 0.0 all-gather.13.cloned.1.call-start
  9.5 0.5 all-gather.13.cloned.1.call-update
  10.1 0.0 reduce-scatter.7.cloned.1.call-start
  10.1 0.0 copy-done.9
  10.1 0.3 dynamic-update-slice.9
  10.4 0.2 dynamic-update-slice.10
  10.6 0.2 dynamic-update-slice.11
  10.8 0.2 dynamic-update-slice.12
  11.0 0.2 dynamic-update-slice.13
  11.3 0.2 dynamic-update-slice.14
  11.5 0.2 dynamic-update-slice.15
  11.7 0.2 dynamic-update-slice.16
  12.0 5.5 all-gather.1
  17.5 0.6 copy.30
  18.1 0.6 copy.31
  19.4 0.6 copy.33
  20.0 0.6 copy.34
  20.5 0.6 copy.35
  21.1 0.6 copy.37
  21.7 0.6 copy.36
  22.4 0.6 fusion.ba_ref
  23.0 38.7 %all-gather.7.cloned.1.call-done.wa_ref = bf16[768,2304]{1,0:T(8,128)(2,1)} async-done(((bf16[384,2304]{1,0:T(8,128)(2,1)}), bf16[768,2304]{1,0:T(8,128)(2,1)}) %all-gather.7.cloned.1.call-update) | async-done | bytes 3538960 | tf_op jit(solution)/shard_map/all_gather | solution.py:374
  61.7 29.3 %front.1 = (bf16[1024,768]{1,0:T(8,128)(2,1)}, bf16[1024,2304]{1,0:T(8,128)(2,1)}, bf16[1024,768]{1,0:T(8,128)(2,1)}, bf16[1024,128]{1,0:T(8,128)(2,1)}) custom-call(s32[1]{0:T(128)S(6)} %copy.61.len_ref, bf16[1024,768]{1,0:T(8,128)(2,1)} %x_ref.5, f32[1,768]{1,0:T(1,128)} %bitcast.42, f32[1,768]{1,0:T(1,128)} %bitcast.48, ...), custom_call_target="tpu_custom_call" | custom-call | flops 7000000000 | bytes 10000000 | tf_op jit(solution)/shard_map/front/pallas_call | solution.py:187
  91.0 59.3 %all-gather.11.cloned.1.call-done.w1_any = bf16[768,3072]{1,0:T(8,128)(2,1)} async-done(((bf16[384,3072]{1,0:T(8,128)(2,1)}), bf16[768,3072]{1,0:T(8,128)(2,1)}) %all-gather.11.cloned.1.call-update) | async-done | bytes 4718608 | tf_op jit(solution)/shard_map/all_gather | solution.py:374
  150.3 64.1 %all-gather.13.cloned.1.call-done.w2_any = bf16[3072,768]{1,0:T(8,128)(2,1)} async-done(((bf16[1536,768]{1,0:T(8,128)(2,1)}), bf16[3072,768]{1,0:T(8,128)(2,1)}) %all-gather.13.cloned.1.call-update) | async-done | bytes 4718608 | tf_op jit(solution)/shard_map/all_gather | solution.py:374
  214.3 61.7 %middle.1 = (bf16[1024,768]{1,0:T(8,128)(2,1)}, f32[1024,768]{1,0:T(8,128)}, bf16[1024,768]{1,0:T(8,128)(2,1)}, bf16[1024,128]{1,0:T(8,128)(2,1)}, bf16[768,3072...) custom-call(s32[1]{0:T(128)S(6)} %copy.61.len_ref, ...), custom_call_target="tpu_custom_call" | custom-call | flops 32999999488 | bytes 30000000 | tf_op jit(solution)/shard_map/middle/pallas_call | solution.py:290
  276.0 0.0 reduce-scatter.7.cloned.1.call-update
  276.1 0.0 reduce-scatter.5.cloned.1.call-start
  276.1 48.6 %back.1 = (bf16[1024,768]{1,0:T(8,128)(2,1)}, bf16[768,2304]{1,0:T(8,128)(2,1)}, f32[1,2304]{1,0:T(1,128)}, f32[2,768]{1,0:T(2,128)}) custom-call(s32[1]{0:T(128)S(6)} %copy.61.len_ref, bf16[1024,2304]{1,0:T(8,128)(2,1)} %get-tuple-element.33.qkv_ref, bf16[1024,768]{1,0:T(8,128)(2,1)} %get-tuple-element.34.do_ref, ...), custom_call_target="tpu_custom_call" | custom-call | flops 16000000000 | bytes 20000000 | tf_op jit(solution)/shard_map/back/pallas_call | solution.py:355
  324.7 0.0 reduce-scatter.5.cloned.1.call-update
  324.7 0.0 reduce-scatter.11.cloned.1.call-start
  324.7 0.7 reduce-scatter.11.cloned.1.call-update
  325.5 0.0 reduce-scatter.9.cloned.1.call-start
  325.5 0.7 reduce-scatter.9.cloned.1.call-update
  326.2 0.0 all-reduce.3.cloned.1.call-start
  326.2 0.0 reduce-scatter.7.cloned.1.call-done
  326.3 46.3 %reduce-scatter.5.cloned.1.call-done = bf16[384,2304]{1,0:T(8,128)(2,1)} async-done(((bf16[768,2304]{1,0:T(8,128)(2,1)}), bf16[384,2304]{1,0:T(8,128)(2,1)}) %reduce-scatter.5.cloned.1.call-update) | async-done | bytes 1769488 | tf_op jit(solution)/shard_map/reduce_scatter | solution.py:391
  372.5 62.3 %reduce-scatter.11.cloned.1.call-done = bf16[1536,768]{1,0:T(8,128)(2,1)} async-done(((bf16[3072,768]{1,0:T(8,128)(2,1)}), bf16[1536,768]{1,0:T(8,128)(2,1)}) %reduce-scatter.11.cloned.1.call-update) | async-done | bytes 2359312 | tf_op jit(solution)/shard_map/reduce_scatter | solution.py:391
  434.9 63.0 %reduce-scatter.9.cloned.1.call-done = bf16[384,3072]{1,0:T(8,128)(2,1)} async-done(((bf16[768,3072]{1,0:T(8,128)(2,1)}), bf16[384,3072]{1,0:T(8,128)(2,1)}) %reduce-scatter.9.cloned.1.call-update) | async-done | bytes 2359312 | tf_op jit(solution)/shard_map/reduce_scatter | solution.py:391
  497.9 0.0 all-reduce.3.cloned.1.call-update
  497.9 0.6 copy-done.5
  498.6 0.0 copy-done.6
  498.8 41.4 %psum.35 = f32[9216]{0:T(1024)S(1)} all-reduce(f32[9216]{0:T(1024)S(1)} %constant_dynamic-update-slice_fusion), channel_id=1, replica_groups=mesh['shard'=2,'rep'=16] {'shard','rep'}, use_global_device_ids=true, to_apply=%region_0.0 | all-reduce | flops 9216 | bytes 73728 | tf_op jit(solution)/shard_map/psum | solution.py:397
  540.3 0.7 dynamic_slice.27
  540.9 0.6 dynamic_slice.28
  541.6 0.6 dynamic_slice.29
  542.2 0.6 dynamic_slice.31
  542.9 0.6 dynamic_slice.25
  543.5 0.6 dynamic_slice.24
  544.2 0.7 dynamic_slice.30
  544.9 0.7 dynamic_slice.26
  545.5 109.0 %all-reduce.3.cloned.1.call-done = (bf16[384,2304]{1,0:T(8,128)(2,1)}, bf16[384,768]{1,0:T(8,128)(2,1)}, bf16[384,3072]{1,0:T(8,128)(2,1)}, bf16[1536,768]{1,0:T(8,128)(2,1)}) async-done(((bf16[384,2304]{1,0:T(8,128)(2,1)}, bf16[384,768]{1,0:T(8,128)(2,1)}, bf16[384,3072]{1,0:T(8,128)(2,1)}, bf16[1536,768]{1,0:T(8,128)(2,1)}), (bf16[384,2304]{1,0:T(8,128)(2,1)}, bf16[384,768]{1,0:T(8,128)(2,1)}, ...) | async-done | bytes 7077904 | tf_op jit(solution)/shard_map/psum | solution.py:392
  654.5 4.6 convert_element_type.79
  659.1 2.5 convert_element_type.80
  661.6 2.0 convert_element_type.77
  663.7 0.0 copy-done.2
  663.7 1.1 convert_element_type.78
  (51 shorter events, 0.3 us)
Async XLA Ops:
  7.2 54.5 %all-gather.7.cloned.1.call-start = ((), (), s32[]{:S(2)}) async-start(), calls=%async_computation.4 | async-start | bytes 5308416 | tf_op jit(solution)/shard_map/all_gather | solution.py:374
  7.9 83.1 %all-gather.9.cloned.1.call-start = ((), (), s32[]{:S(2)}) async-start(), calls=%async_computation.5 | async-start | bytes 1769472 | tf_op jit(solution)/shard_map/all_gather | solution.py:374
  8.7 1.4 copy-start.9
  8.7 1.7 copy-start.10
  8.7 1.9 copy-start.8
  8.7 2.1 copy-start.11
  8.7 2.3 copy-start.12
  8.7 2.5 copy-start.13
  8.7 2.8 copy-start.7
  8.7 3.0 copy-start.14
  8.7 141.5 %all-gather.11.cloned.1.call-start = ((), (), s32[]{:S(2)}) async-start(), calls=%async_computation.6 | async-start | bytes 7077888 | tf_op jit(solution)/shard_map/all_gather | solution.py:374
  9.5 204.9 %all-gather.13.cloned.1.call-start = ((), (), s32[]{:S(2)}) async-start(), calls=%async_computation.7 | async-start | bytes 7077888 | tf_op jit(solution)/shard_map/all_gather | solution.py:374
  10.1 316.2 %reduce-scatter.7.cloned.1.call-start = ((), (), s32[]{:S(2)}) async-start(), calls=%async_computation.9 | async-start | bytes 1769472 | tf_op jit(solution)/shard_map/reduce_scatter | solution.py:391
  276.1 96.5 %reduce-scatter.5.cloned.1.call-start = ((), (), s32[]{:S(2)}) async-start(), calls=%async_computation.8 | async-start | bytes 5308416 | tf_op jit(solution)/shard_map/reduce_scatter | solution.py:391
  324.7 110.2 %reduce-scatter.11.cloned.1.call-start = ((), (), s32[]{:S(2)}) async-start(), calls=%async_computation.11 | async-start | bytes 7077888 | tf_op jit(solution)/shard_map/reduce_scatter | solution.py:391
  325.5 172.4 %reduce-scatter.9.cloned.1.call-start = ((), (), s32[]{:S(2)}) async-start(), calls=%async_computation.10 | async-start | bytes 7077888 | tf_op jit(solution)/shard_map/reduce_scatter | solution.py:391
  326.2 328.3 %all-reduce.3.cloned.1.call-start = ((), (), s32[]{:S(2)}) async-start(), calls=%async_computation.12 | async-start | bytes 14155776 | tf_op jit(solution)/shard_map/psum | solution.py:392
  497.9 0.7 copy-start.5
  497.9 0.7 copy-start.6
  497.9 0.8 copy-start.3
  497.9 0.9 copy-start.4
  654.5 4.6 copy-start
  659.1 2.5 copy-start.1
  661.6 2.0 copy-start.2
Sparse Core Ops, SparseCore 0:
  9.6 52.0 all-gather.6
  63.2 22.7 all-gather.8
  87.6 62.6 all-gather.10
  151.6 62.6 all-gather.12
  276.2 21.7 reduce-scatter.6
  324.8 47.6 reduce-scatter.4
  374.8 59.9 reduce-scatter.10
  437.8 59.9 reduce-scatter.8
  501.9 152.5 all-reduce.2

commit v2 on v1

--- a/solution.py
+++ b/solution.py
@@ -56,9 +56,9 @@
 def fwd_pair(hp, length, qkv_ref, o_ref, lse_ref):
     QB = 512
     cq = pl.multiple_of(hp * 128, 128)
-    q = qkv_ref[:, pl.ds(cq, 128)]
-    k = qkv_ref[:, pl.ds(pl.multiple_of(cq + D, 128), 128)]
-    v = qkv_ref[:, pl.ds(pl.multiple_of(cq + 2 * D, 128), 128)]
+    q = qkv_ref[0:SEQ, pl.ds(cq, 128)]
+    k = qkv_ref[SEQ : 2 * SEQ, pl.ds(cq, 128)]
+    v = qkv_ref[2 * SEQ : 3 * SEQ, pl.ds(cq, 128)]
     vt = v.T
     ln = lanes((SEQ, 128))
     rw = rowsi((SEQ, 128))
@@ -100,11 +100,9 @@
 def bwd_pair(hp, length, qkv_ref, do_ref, augq_ref, augd_ref, dqkv_ref):
     KB = 512
     cq = pl.multiple_of(hp * 128, 128)
-    ck = pl.multiple_of(cq + D, 128)
-    cv = pl.multiple_of(cq + 2 * D, 128)
-    q = qkv_ref[:, pl.ds(cq, 128)]
-    k = qkv_ref[:, pl.ds(ck, 128)]
-    v = qkv_ref[:, pl.ds(cv, 128)]
+    q = qkv_ref[0:SEQ, pl.ds(cq, 128)]
+    k = qkv_ref[SEQ : 2 * SEQ, pl.ds(cq, 128)]
+    v = qkv_ref[2 * SEQ : 3 * SEQ, pl.ds(cq, 128)]
     do = do_ref[:, pl.ds(cq, 128)]
     qt = q.T
     dot_ = do.T
@@ -147,9 +145,19 @@
         if h == 1:
             dkp = jnp.concatenate([dk[(kb, 0)], dk[(kb, 1)]], axis=0).astype(bf)
             dvp = jnp.concatenate([dv[(kb, 0)], dv[(kb, 1)]], axis=0).astype(bf)
-            dqkv_ref[kb * KB : (kb + 1) * KB, pl.ds(ck, 128)] = dkp.T
-            dqkv_ref[kb * KB : (kb + 1) * KB, pl.ds(cv, 128)] = dvp.T
-    dqkv_ref[:, pl.ds(cq, 128)] = (jnp.where(lanes((SEQ, 128)) < 64, dq[0], dq[1]) * 0.125).astype(bf)
+            dqkv_ref[SEQ + kb * KB : SEQ + (kb + 1) * KB, pl.ds(cq, 128)] = dkp.T
+            dqkv_ref[2 * SEQ + kb * KB : 2 * SEQ + (kb + 1) * KB, pl.ds(cq, 128)] = dvp.T
+    dqkv_ref[0:SEQ, pl.ds(cq, 128)] = (jnp.where(lanes((SEQ, 128)) < 64, dq[0], dq[1]) * 0.125).astype(bf)
+
+
+def project(h_ref, wa_ref, bias, qkv_ref):
+    for i in range(3):
+        t = dot(h_ref[...], wa_ref[:, i * D : (i + 1) * D])
+        if bias(i) is not None:
+            t = t + bias(i)
+        if i == 0:
+            t = t.astype(bf).astype(f32) * 0.125
+        qkv_ref[i * SEQ : (i + 1) * SEQ, :] = t.astype(bf)
 
 
 def front_kernel(len_ref, x_ref, g_ref, b_ref, wa_ref, ba_ref, h_ref, qkv_ref, o_ref, aug_ref, lse_ref):
@@ -163,14 +171,7 @@
 
     lax.fori_loop(0, SEQ // RB, rows, 0)
 
-    def cols(j, _):
-        c = pl.ds(pl.multiple_of(j * 256, 256), 256)
-        t = dot(h_ref[...], wa_ref[:, c]) + ba_ref[:, c]
-        t = t.astype(bf).astype(f32) * jnp.where(j < D // 256, 0.125, 1.0)
-        qkv_ref[:, c] = t.astype(bf)
-        return 0
-
-    lax.fori_loop(0, 3 * D // 256, cols, 0)
+    project(h_ref, wa_ref, lambda i: ba_ref[:, i * D : (i + 1) * D], qkv_ref)
     lse_ref[...] = jnp.zeros_like(lse_ref)
 
     def pair(hp, _):
@@ -188,7 +189,7 @@
         front_kernel,
         out_shape=(
             jax.ShapeDtypeStruct((SEQ, D), bf),
-            jax.ShapeDtypeStruct((SEQ, 3 * D), bf),
+            jax.ShapeDtypeStruct((3 * SEQ, D), bf),
             jax.ShapeDtypeStruct((SEQ, D), bf),
             jax.ShapeDtypeStruct((SEQ, 128), bf),
         ),
@@ -320,7 +321,7 @@
 
 
 def back_kernel(len_ref, qkv_ref, do_ref, augq_ref, augd_ref, h_ref, x_ref, dx_ref, g_ref, wa_ref,
-                ts_ref, dwa_ref, dba_ref, dsm_ref, dqkv_ref, dh_ref):
+                ts_ref, dwa_ref, dba_ref, dsm_ref, dqkv_ref):
     length = len_ref[0]
 
     def pair(hp, _):
@@ -329,18 +330,17 @@
 
     lax.fori_loop(0, H // 2, pair, 0)
 
-    def cols(j, _):
-        c = pl.ds(pl.multiple_of(j * 256, 256), 256)
-        d = dqkv_ref[:, c]
-        dba_ref[:, c] = jnp.sum(d.astype(f32), axis=0, keepdims=True)
-        dwa_ref[:, c] = dot(h_ref[...], d, TN).astype(bf)
-        return 0
-
-    lax.fori_loop(0, 3 * D // 256, cols, 0)
+    for i in range(3):
+        d = dqkv_ref[i * SEQ : (i + 1) * SEQ, :]
+        dba_ref[:, i * D : (i + 1) * D] = jnp.sum(d.astype(f32), axis=0, keepdims=True)
+        dwa_ref[:, i * D : (i + 1) * D] = dot(h_ref[...], d, TN).astype(bf)
 
     def rows(i, acc):
         r = pl.ds(pl.multiple_of(i * RB, RB), RB)
-        dh = dot(dqkv_ref[r, :], wa_ref[...], NT)
+        dh = jnp.zeros((RB, D), f32)
+        for k in range(3):
+            d = dqkv_ref[pl.ds(pl.multiple_of(i * RB + k * SEQ, RB), RB), :]
+            dh = dh + dot(d, wa_ref[:, k * D : (k + 1) * D], NT)
         n, rs = norm(x_ref[r, :].astype(f32))
         ts_ref[r, :] = (dx_ref[r, :] + norm_back(dh, n, rs, g_ref[...])).astype(bf)
         return acc[0] + jnp.sum(dh * n, axis=0, keepdims=True), acc[1] + jnp.sum(dh, axis=0, keepdims=True)
@@ -362,14 +362,14 @@
         ),
         in_specs=[SM] + [VM] * 9,
         out_specs=(VM,) * 4,
-        scratch_shapes=[pltpu.VMEM((SEQ, 3 * D), bf), pltpu.VMEM((SEQ, D), f32)],
+        scratch_shapes=[pltpu.VMEM((3 * SEQ, D), bf)],
         compiler_params=pltpu.CompilerParams(vmem_limit_bytes=VLIMIT),
         cost_estimate=pl.CostEstimate(flops=16 * 10**9, bytes_accessed=2 * 10**7, transcendentals=12 * 2**20),
         name="back",
     )(length, qkv, do, augq, augd, h1, x, dx, g1, wa)
 
 
-def shards(x, lengths, cot, g1, b1, wa, ba, wo, bo, g2, b2, w1, be, w2, br):
+def plain_shards(x, lengths, cot, g1, b1, wa, ba, wo, bo, g2, b2, w1, be, w2, br):
     def gather(v):
         return lax.all_gather(v, "shard", axis=0, tiled=True)
 
@@ -413,10 +413,502 @@
     )
 
 
+MESH = pl.DeviceIdType.MESH
+HF = D // 2
+NCHUNK = 12
+G1, B1, BA, BO, G2, B2, BE, BR = 0, 1, 2, 4, 5, 6, 7, 11
+
+
+class Place:
+    def __init__(self):
+        s = lax.axis_index("shard")
+        r = lax.axis_index("rep")
+        core = r % 2
+        x = (r // 2) % 2
+        z = r // 4
+        self.s, self.core, self.x, self.a, self.b = s, core, x, (z % 2 + z // 2) % 2, z // 2
+        self.to = {
+            "core": (s, r + 1 - 2 * core),
+            "y": (1 - s, r),
+            "x": (s, r + 2 - 4 * x),
+            "a": (s, r + 4 - 8 * (z % 2)),
+            "b": (s, r + 4 * (3 - 2 * z)),
+        }
+
+    def greet(self):
+        barrier = pltpu.get_barrier_semaphore()
+        for d in self.to.values():
+            pl.semaphore_signal(barrier, inc=1, device_id=d, device_id_type=MESH)
+        pl.semaphore_wait(barrier, len(self.to))
+
+
+def remote(src, dst, send, recv, to):
+    return pltpu.make_async_remote_copy(
+        src_ref=src, dst_ref=dst, send_sem=send, recv_sem=recv, device_id=to, device_id_type=MESH
+    )
+
+
+class Unit:
+    def __init__(self, place, index, own, full, r0, nr, c0, width, send, recv):
+        self.p, self.i, self.own, self.full = place, index, own, full
+        self.r0, self.n, self.half = r0, nr // 8, own.shape[0]
+        w = width // 2
+        self.cols = [pl.ds(c0, w), pl.ds(c0 + w, w)]
+        self.send, self.recv = send, recv
+
+    def copies(self, step):
+        p, n = self.p, self.n
+        out = []
+        for k, zc in enumerate((p.a, p.b)):
+            spot = p.core * 4 + zc * 2 + p.x
+            other = (1 - p.s) * self.half + self.r0
+            sems = (self.send.at[self.i, step, k], self.recv.at[self.i, step, k])
+            if step == 0:
+                src = self.own.at[pl.ds(pl.multiple_of(self.r0 + spot * n, 16), n), self.cols[k]]
+                dst = self.full.at[pl.ds(pl.multiple_of(p.s * self.half + self.r0 + spot * n, 16), n), self.cols[k]]
+                out.append(remote(src, dst, *sems, p.to["y"]))
+                continue
+            if step == 1:
+                at, m, to = spot, 1, p.to["x"]
+            elif step == 2:
+                at, m, to = p.core * 4 + zc * 2, 2, p.to["ab"[k]]
+            else:
+                at, m, to = p.core * 4, 4, p.to["core"]
+            ref = self.full.at[pl.ds(pl.multiple_of(other + at * n, 16), m * n), self.cols[k]]
+            out.append(remote(ref, ref, *sems, to))
+        return out
+
+    def start(self, step):
+        for c in self.copies(step):
+            c.start()
+
+    def wait(self, step):
+        for c in self.copies(step):
+            c.wait()
+
+    def move(self, step):
+        self.wait(step - 1)
+        if step < 4:
+            self.start(step)
+
+
+def vec(sm_ref, row, rows=1):
+    return jnp.concatenate([sm_ref[0, row : row + rows], sm_ref[1, row : row + rows]], axis=1)
+
+
+def lead_kernel(
+    len_ref, x_ref, sm_own, wa_own, wo_own, w1_own, w2_own,
+    h_ref, qkv_ref, o_ref, aug_ref, wa_ref, sm_ref, wo_ref, w1_ref, w2_ref,
+    lse_ref, send, recv, sm_send, sm_recv, lsem,
+):
+    place = Place()
+    length = len_ref[0]
+    s = place.s
+    local = []
+    for i, (own, full) in enumerate(((wa_own, wa_ref), (wo_own, wo_ref), (w1_own, w1_ref), (w2_own, w2_ref))):
+        m = own.shape[0]
+        local.append(pltpu.make_async_copy(own, full.at[pl.ds(pl.multiple_of(s * m, 16), m)], lsem.at[i]))
+    local.append(pltpu.make_async_copy(sm_own, sm_ref.at[s], lsem.at[4]))
+    for c in local:
+        c.start()
+    specs = [(wa_own, wa_ref, 0, HF, i * D, D) for i in range(3)]
+    specs += [(wo_own, wo_ref, 0, HF, 0, D), (w1_own, w1_ref, 0, HF, 0, 2 * D)]
+    specs += [(w1_own, w1_ref, 0, HF, 2 * D, 2 * D), (w2_own, w2_ref, 0, D, 0, D)]
+    specs += [(w2_own, w2_ref, D, D, 0, D)]
+    units = [Unit(place, i, *t, send, recv) for i, t in enumerate(specs)]
+    groups = [units[3:5], units[5:7], units[7:8]]
+    place.greet()
+    smc = remote(sm_own, sm_ref.at[s], sm_send, sm_recv, place.to["y"])
+    smc.start()
+    for u in units[:3]:
+        u.start(0)
+    local[4].wait()
+    smc.wait()
+    g1, b1 = vec(sm_ref, G1), vec(sm_ref, B1)
+
+    def rows(i, _):
+        r = pl.ds(pl.multiple_of(i * RB, RB), RB)
+        n, _r = norm(x_ref[r, :].astype(f32))
+        h_ref[r, :] = (n * g1 + b1).astype(bf)
+        return 0
+
+    lax.fori_loop(0, SEQ // RB, rows, 0)
+    for u in units[:3]:
+        u.move(1)
+    for u in units[3:]:
+        u.start(0)
+    for u in units[:3]:
+        u.move(2)
+    for u in units[:3]:
+        u.move(3)
+    for u in units[:3]:
+        u.move(4)
+    local[0].wait()
+    bias = [
+        jnp.concatenate([sm_ref[0, BA : BA + 1], sm_ref[0, BA + 1 : BA + 2]], axis=1),
+        None,
+        jnp.concatenate([sm_ref[1, BA : BA + 1], sm_ref[1, BA + 1 : BA + 2]], axis=1),
+    ]
+    project(h_ref, wa_ref, lambda i: bias[i], qkv_ref)
+    lse_ref[...] = jnp.zeros_like(lse_ref)
+
+    def go(group, step):
+        for u in groups[group]:
+            u.move(step)
+
+    go(0, 1)
+
+    def pair(hp, _):
+        fwd_pair(hp, length, qkv_ref, o_ref, lse_ref)
+        for t in range(5):
+
+            @pl.when(hp == t)
+            def _(t=t):
+                for group in range(3):
+                    step = t + 2 - group
+                    if 1 <= step <= 4:
+                        go(group, step)
+
+        return 0
+
+    lax.fori_loop(0, H // 2, pair, 0)
+    hi, mid, lo = three(lse_ref[...])
+    one = jnp.where(rowsi((80, SEQ)) == 0, 1.0, 0.0)
+    aug_ref[...] = jnp.concatenate([hi, mid, lo, one], axis=0).astype(bf).T
+    for c in local[1:4]:
+        c.wait()
+
+
+def lead(length, x, sm, wa, wo, w1, w2):
+    sds = jax.ShapeDtypeStruct
+    return pl.pallas_call(
+        lead_kernel,
+        out_shape=(
+            sds((SEQ, D), bf),
+            sds((3 * SEQ, D), bf),
+            sds((SEQ, D), bf),
+            sds((SEQ, 128), bf),
+            sds((D, 3 * D), bf),
+            sds((2, 16, HF), f32),
+            sds((D, D), bf),
+            sds((D, FF), bf),
+            sds((FF, D), bf),
+        ),
+        in_specs=[SM, VM, VM] + [HB] * 4,
+        out_specs=(VM,) * 6 + (HB,) * 3,
+        scratch_shapes=[
+            pltpu.VMEM((16, SEQ), f32),
+            pltpu.SemaphoreType.DMA((8, 4, 2)),
+            pltpu.SemaphoreType.DMA((8, 4, 2)),
+            pltpu.SemaphoreType.DMA(()),
+            pltpu.SemaphoreType.DMA(()),
+            pltpu.SemaphoreType.DMA((5,)),
+        ],
+        compiler_params=pltpu.CompilerParams(vmem_limit_bytes=VLIMIT, collective_id=0, has_side_effects=True),
+        cost_estimate=pl.CostEstimate(flops=7 * 10**9, bytes_accessed=10**7, transcendentals=12 * 2**20),
+        name="lead",
+    )(length, x, sm, wa, wo, w1, w2)
+
+
+class Reduce:
+    STEPS = ("core", "y", "x", "a", "b", "b", "a", "x", "core")
+
+    def __init__(self, place, first, sums, lands, total, send, recv, keep_sem):
+        self.p, self.f, self.k, self.l, self.g = place, first, sums, lands, total
+        self.send, self.recv, self.keep_sem = send, recv, keep_sem
+
+    def rows(self, at, n):
+        return pl.ds(pl.multiple_of(at, 16), n)
+
+    def copy(self, step, c):
+        p, slot, two = self.p, c % 4, c % 2
+        sems = (self.send.at[step, slot], self.recv.at[step, slot], p.to[self.STEPS[step]])
+        if step == 0:
+            return remote(self.f.at[two, 1 - p.core], self.l[0].at[slot], *sems)
+        if step < 5:
+            n = D >> step
+            away = 1 - (p.s, p.x, p.a, p.b)[step - 1]
+            return remote(self.k[step - 1].at[two, self.rows(away * n, n)], self.l[step].at[slot], *sems)
+        base = p.core * HF
+        if step == 5:
+            at = base + (p.x * 4 + p.a * 2 + p.b) * 48
+            return remote(self.k[4].at[two], self.g.at[c, self.rows(at, 48)], *sems)
+        if step == 6:
+            at, n = base + (p.x * 4 + p.a * 2) * 48, 96
+        elif step == 7:
+            at, n = base + p.x * 192, 192
+        else:
+            at, n = base, HF
+        ref = self.g.at[c, self.rows(at, n)]
+        return remote(ref, ref, *sems)
+
+    def keep(self, c):
+        p = self.p
+        at = p.core * HF + (p.x * 4 + p.a * 2 + p.b) * 48
+        return pltpu.make_async_copy(self.k[4].at[c % 2], self.g.at[c, self.rows(at, 48)], self.keep_sem.at[c % 2])
+
+    def stage(self, step, c):
+        p, slot, two = self.p, c % 4, c % 2
+        if step > 0:
+            self.copy(step - 1, c).wait()
+        if 1 <= step <= 5:
+            n = D >> (step - 1)
+            if step == 1:
+                mine = self.f[two, p.core]
+            else:
+                bit = (p.s, p.x, p.a, p.b)[step - 2]
+                mine = self.k[step - 2][two, self.rows(bit * n, n)]
+            self.k[step - 1][two] = (mine.astype(f32) + self.l[step - 1][slot].astype(f32)).astype(bf)
+        if step == 5:
+            self.keep(c).start()
+        if step == 6:
+            self.keep(c).wait()
+        if step < 9:
+            self.copy(step, c).start()
+
+    def tick(self, t):
+        for step in range(9, -1, -1):
+            e = t - step
+            if isinstance(e, int):
+                if 0 <= e <= 14 and (e <= 8 or e % 2 == 0):
+                    self.stage(step, e if e <= 8 else 4 + e // 2)
+                continue
+
+            @pl.when((e >= 0) & (e <= 14) & ((e <= 8) | (e % 2 == 0)))
+            def _(step=step, e=e):
+                self.stage(step, jnp.where(e <= 8, e, 4 + e // 2))
+
+
+def rest_kernel(
+    len_ref, sm_ref, x_any, o_any, cot_any, h1_any, qkv_any, augq_ref, wo_any, wa_any, w1_any, w2_any,
+    out_any, ts_any, g_any, sv_ref,
+    m1, m2, wo, wa, t1, t2, o_ref, gb_ref, h_ref, dxb_ref, do_ref, augd_ref, x1_ref, y_ref, dh_ref,
+    first, k0, k1, k2, k3, k4, l0, l1, l2, l3, l4, sva, svl,
+    lsem, osem, send, recv, keep_sem, svs, svr,
+):
+    place = Place()
+    red = Reduce(place, first, (k0, k1, k2, k3, k4), (l0, l1, l2, l3, l4), g_any, send, recv, keep_sem)
+    length = len_ref[0]
+
+    def load(i, src, dst):
+        c = pltpu.make_async_copy(src, dst, lsem.at[i])
+        c.start()
+        return c
+
+    early = [load(0, x_any, t1), load(1, o_any, o_ref), load(2, cot_any, gb_ref), load(3, wo_any, wo)]
+    weights = []
+    for j in range(4):
+        for h in range(2):
+            away = pl.ds(j * D + h * HF, HF)
+            near = pl.ds(h * (FF // 2) + j * HF, HF)
+            weights.append(load(4 + 4 * j + 2 * h, w1_any.at[:, near], m1.at[pl.ds(j * D, D), pl.ds(h * HF, HF)]))
+            weights.append(load(5 + 4 * j + 2 * h, w2_any.at[near, :], m2.at[away, :]))
+    place.greet()
+    wal = load(20, wa_any, wa)
+    for c in early:
+        c.wait()
+    bo, g2, b2, br = vec(sm_ref, BO), vec(sm_ref, G2), vec(sm_ref, B2), vec(sm_ref, BR)
+
+    def rows1(i, acc):
+        r = pl.ds(pl.multiple_of(i * RB, RB), RB)
+        x1 = t1[r, :].astype(f32) + (dot(o_ref[r, :], wo[...]) + bo)
+        x1_ref[r, :] = x1
+        y_ref[r, :] = x1 + br
+        n, _r = norm(x1)
+        h_ref[r, :] = (n * g2 + b2).astype(bf)
+        live = (rowsi((RB, 1)) + i * RB) < length
+        gb = jnp.where(live, gb_ref[r, :].astype(f32), 0.0)
+        gb_ref[r, :] = gb.astype(bf)
+        dh_ref[r, :] = jnp.zeros((RB, D), f32)
+        return acc + jnp.sum(gb, axis=0, keepdims=True)
+
+    sva[0, 12:16, :] = jnp.zeros((4, D), f32)
+    sva[0, 7:8, :] = lax.fori_loop(0, SEQ // RB, rows1, jnp.zeros((1, D), f32))
+    for c in weights:
+        c.wait()
+
+    def emit(c, value):
+        for h in range(2):
+            first[c % 2, h] = value[:, h * HF : (h + 1) * HF].astype(bf)
+
+    def hidden(j, _):
+        rj = pl.ds(pl.multiple_of(j * D, D), D)
+        be = jnp.concatenate([sm_ref[0, pl.ds(BE + j, 1), :], sm_ref[1, pl.ds(BE + j, 1), :]], axis=1)
+        NB = 512
+
+        def rows2(i, acc):
+            r = pl.ds(pl.multiple_of(i * NB, NB), NB)
+            u = dot(h_ref[r, :], m1[rj, :]) + be
+            sig = 0.5 * jnp.tanh(0.851 * u) + 0.5
+            a = u * sig
+            ab = a.astype(bf)
+            t1[r, :] = ab
+            y_ref[r, :] += dot(ab, m2[rj, :])
+            da = dot(gb_ref[r, :], m2[rj, :], NT)
+            du = da * (sig * (1.0 + 1.702 * (u - a)))
+            dub = du.astype(bf)
+            t2[r, :] = dub
+            dh_ref[r, :] += dot(dub, m1[rj, :], NT)
+            return acc + jnp.sum(du, axis=0, keepdims=True)
+
+        sva[0, pl.ds(8 + j, 1), :] = lax.fori_loop(0, SEQ // NB, rows2, jnp.zeros((1, D), f32))
+        emit(0, dot(t1[...], gb_ref[...], TN))
+        red.tick(2 * j)
+        emit(1, dot(h_ref[...], t2[...], TN))
+        red.tick(2 * j + 1)
+        return 0
+
+    lax.fori_loop(0, 4, hidden, 0)
+    late = [load(0, qkv_any, m1), load(1, h1_any, h_ref), load(2, x_any, t2)]
+    ln = lanes((RB, 128))
+    sel = ((lanes((D, 128)) % 16 == rowsi((D, 128)) // 64) & (lanes((D, 128)) < 48)).astype(f32).astype(bf)
+
+    def rows3(i, acc):
+        r = pl.ds(pl.multiple_of(i * RB, RB), RB)
+        x1 = x1_ref[r, :]
+        live = (rowsi((RB, 1)) + i * RB) < length
+        t1[r, :] = jnp.where(live, y_ref[r, :], 0.0).astype(bf)
+        n, rs = norm(x1)
+        dh = dh_ref[r, :]
+        dx = gb_ref[r, :].astype(f32) + norm_back(dh, n, rs, g2)
+        x1_ref[r, :] = dx
+        dxb = dx.astype(bf)
+        dxb_ref[r, :] = dxb
+        do = dot(dxb, wo[...], NT).astype(bf)
+        do_ref[r, :] = do
+        prod = do.astype(f32) * o_ref[r, :].astype(f32)
+        phi = prod.astype(bf)
+        dl = dot(phi, sel) + dot((prod - phi.astype(f32)).astype(bf), sel)
+        hi, mid, lo = three(dl)
+        augd_ref[r, :] = jnp.where(ln < 16, hi, jnp.where(ln < 32, mid, lo)).astype(bf)
+        return (
+            acc[0] + jnp.sum(dh * n, axis=0, keepdims=True),
+            acc[1] + jnp.sum(dh, axis=0, keepdims=True),
+            acc[2] + jnp.sum(dx, axis=0, keepdims=True),
+        )
+
+    z = jnp.zeros((1, D), f32)
+    a0, a1, a2 = lax.fori_loop(0, SEQ // RB, rows3, (z, z, z))
+    sva[0, 5:6, :] = a0
+    sva[0, 6:7, :] = a1
+    sva[0, 4:5, :] = a2
+    out_copy = pltpu.make_async_copy(t1, out_any, osem.at[0])
+    out_copy.start()
+    emit(0, dot(o_ref[...], dxb_ref[...], TN))
+    red.tick(8)
+    for c in late:
+        c.wait()
+
+    def pair(hp, _):
+        bwd_pair(hp, length, m1, do_ref, augq_ref, augd_ref, m2)
+
+        @pl.when(hp % 2 == 1)
+        def _():
+            c = pl.ds(pl.multiple_of((hp // 2) * 256, 256), 256)
+            parts = [dot(h_ref[...], m2[k * SEQ : (k + 1) * SEQ, c], TN).astype(bf) for k in range(3)]
+            two = (9 + hp // 2) % 2
+            first[two, 0, :, 0:256] = parts[0]
+            first[two, 0, :, 256:384] = parts[1][:, 0:128]
+            first[two, 1, :, 0:128] = parts[1][:, 128:256]
+            first[two, 1, :, 128:384] = parts[2]
+
+        red.tick(9 + hp)
+        return 0
+
+    lax.fori_loop(0, H // 2, pair, 0)
+    for k, row in ((0, 2), (2, 3)):
+        sva[0, row : row + 1, :] = jnp.sum(m2[k * SEQ : (k + 1) * SEQ, :].astype(f32), axis=0, keepdims=True)
+    wal.wait()
+    g1 = vec(sm_ref, G1)
+
+    def rows4(i, acc):
+        r = pl.ds(pl.multiple_of(i * RB, RB), RB)
+        dh = jnp.zeros((RB, D), f32)
+        for k in range(3):
+            d = m2[pl.ds(pl.multiple_of(i * RB + k * SEQ, RB), RB), :]
+            dh = dh + dot(d, wa[:, k * D : (k + 1) * D], NT)
+        n, rs = norm(t2[r, :].astype(f32))
+        gb_ref[r, :] = (x1_ref[r, :] + norm_back(dh, n, rs, g1)).astype(bf)
+        red.tick(15 + i)
+        return acc[0] + jnp.sum(dh * n, axis=0, keepdims=True), acc[1] + jnp.sum(dh, axis=0, keepdims=True)
+
+    a0, a1 = lax.fori_loop(0, SEQ // RB, rows4, (z, z))
+    sva[0, 0:1, :] = a0
+    sva[0, 1:2, :] = a1
+    ts_copy = pltpu.make_async_copy(gb_ref, ts_any, osem.at[1])
+    ts_copy.start()
+
+    def sv(step):
+        return remote(sva.at[step], svl.at[step], svs.at[step], svr.at[step], place.to[red.STEPS[step]])
+
+    sv(0).start()
+    for step in range(5):
+        red.tick(19 + step)
+        sv(step).wait()
+        total = sva[step] + svl[step]
+        if step < 4:
+            sva[step + 1] = total
+            sv(step + 1).start()
+        else:
+            sv_ref[...] = total
+    out_copy.wait()
+    ts_copy.wait()
+
+
+def rest(length, sm, x, o, cot, h1, qkv, augq, wo, wa, w1, w2):
+    sds = jax.ShapeDtypeStruct
+    V = pltpu.VMEM
+    dma = pltpu.SemaphoreType.DMA
+    return pl.pallas_call(
+        rest_kernel,
+        out_shape=(
+            sds((SEQ, D), bf),
+            sds((SEQ, D), bf),
+            sds((NCHUNK, D, HF), bf),
+            sds((16, D), f32),
+        ),
+        in_specs=[SM, VM] + [HB] * 5 + [VM] + [HB] * 4,
+        out_specs=(HB, HB, HB, VM),
+        scratch_shapes=[
+            V((FF, D), bf), V((FF, D), bf), V((D, D), bf), V((D, 3 * D), bf),
+            V((SEQ, D), bf), V((SEQ, D), bf), V((SEQ, D), bf), V((SEQ, D), bf), V((SEQ, D), bf),
+            V((SEQ, D), bf), V((SEQ, D), bf), V((SEQ, 128), bf),
+            V((SEQ, D), f32), V((SEQ, D), f32), V((SEQ, D), f32),
+            V((2, 2, D, HF), bf),
+            V((2, D, HF), bf), V((2, 384, HF), bf), V((2, 192, HF), bf), V((2, 96, HF), bf), V((2, 48, HF), bf),
+            V((4, D, HF), bf), V((4, 384, HF), bf), V((4, 192, HF), bf), V((4, 96, HF), bf), V((4, 48, HF), bf),
+            V((5, 16, D), f32), V((5, 16, D), f32),
+            dma((21,)), dma((2,)), dma((9, 4)), dma((9, 4)), dma((2,)), dma((5,)), dma((5,)),
+        ],
+        compiler_params=pltpu.CompilerParams(vmem_limit_bytes=VLIMIT, collective_id=1, has_side_effects=True),
+        cost_estimate=pl.CostEstimate(flops=49 * 10**9, bytes_accessed=5 * 10**7, transcendentals=15 * 2**20),
+        name="rest",
+    )(length, sm, x, o, cot, h1, qkv, augq, wo, wa, w1, w2)
+
+
+def shards(x, lengths, cot, g1, b1, wa, ba, wo, bo, g2, b2, w1, be, w2, br):
+    sm = jnp.concatenate([g1, b1, ba, bo, g2, b2, be, br]).astype(f32).reshape(12, HF)
+    sm = jnp.pad(sm, ((0, 4), (0, 0)))
+    h1, qkv, o, augq, wa, sm, wo, w1, w2 = lead(lengths, x, sm, wa, wo, w1, w2)
+    out, ts, g, sv = rest(lengths, sm, x, o, cot, h1, qkv, augq, wo, wa, w1, w2)
+    me = lax.axis_index("shard")
+    g = g.reshape(NCHUNK, 2, HF, HF)
+    dw2 = g[0:8:2].transpose(0, 2, 1, 3).reshape(FF // 2, D).astype(f32)
+    dw1 = g[1:8:2].transpose(2, 1, 0, 3).reshape(HF, FF).astype(f32)
+    dwo = g[8].transpose(1, 0, 2).reshape(HF, D).astype(f32)
+    dwa = g[9:].transpose(0, 2, 1, 3).reshape(3, HF, 3, 256).transpose(1, 2, 0, 3).reshape(HF, 3 * D).astype(f32)
+    half = lax.dynamic_slice(sv, (0, me * HF), (16, HF))
+    dba = lax.dynamic_slice(sv[2:4], (me, 0), (1, D))[0]
+    return (
+        out, ts, half[0], half[1], dwa, dba, dwo, half[4], half[5], half[6], dw1, half[8:12].reshape(-1), dw2, half[7],
+    )
+
+
 def solution(mesh):
     rows = P(("shard", "rep"), None)
     vec = P("shard")
     mat = P("shard", None)
     in_specs = (rows, P(("shard", "rep")), rows, vec, vec, mat, vec, mat, vec, vec, vec, mat, vec, mat, vec)
     out_specs = (rows, rows, vec, vec, mat, vec, mat, vec, vec, vec, mat, vec, mat, vec)
-    return jax.shard_map(shards, mesh=mesh, in_specs=in_specs, out_specs=out_specs, check_vma=False)
+    body = shards if mesh.shape["shard"] == 2 and mesh.shape["rep"] == 16 else plain_shards
+    return jax.shard_map(body, mesh=mesh, in_specs=in_specs, out_specs=out_specs, check_vma=False)

time: 672 us -> 386 us (0.57)
  waiting for transfers between devices: 447 us -> 0 us
  Pallas kernels: 140 us -> 329 us
  blocking collectives: 47 us -> 0 us
  local copies, waits for them, and re-layouts: 12.1 us -> 43.5 us
  between operations: 14.8 us -> 1.83 us
  other arithmetic: 10.9 us -> 4.06 us
    pallas_call x3 -> x2, Pallas kernels: 140 us -> 329 us  [the longest x1 169 us: lead(): pl.pallas_call(lead_kernel, out_shape=(sds((SEQ, D), bf), sds((3 * SEQ, D...]
    reduce_scatter x4 -> x0, waiting for transfers between devices: 172 us -> none  [reduce_big(): v = lax.psum_scatter(v, 'shard', scatter_dimension=0, tiled=True)]
    all_gather x4 -> x0, waiting for transfers between devices: 162 us -> none  [gather(): return lax.all_gather(v, 'shard', axis=0, tiled=True)]
    psum x1 -> x0, waiting for transfers between devices: 109 us -> none  [reduce_big(): return lax.psum(v, 'rep').astype(f32)]
    psum x1 -> x0, blocking collectives: 41.4 us -> none  [shards(): total = lax.psum(jnp.concatenate(parts), ('shard', 'rep'))]
    convert_element_type x0 -> x7, local copies, waits for them, and re-layouts: none -> 21.2 us  [the longest x2 11.6 us: shards(): dw1 = g[1:8:2].transpose(2, 1, 0, 3).reshape(HF, FF).astype(f32)]
    unnamed x55 -> x15, local copies, waits for them, and re-layouts: 6.52 us -> 14.4 us
    convert_element_type x4 -> x1, other arithmetic: 10.2 us -> 3.37 us  [shards(): dw2 = g[0:8:2].transpose(0, 2, 1, 3).reshape(FF // 2, D).astype(f32)]
  transfers between devices with their start and end apart: 9 -> 0, of which waited for: 7 -> 0; matrix products, arithmetic and copies ran while one was open for 2% -> 0% of each run, Pallas kernels for 12% -> 0%
where the time goes in v2:
time: 386 us; the launch traced here: 379 us
  Pallas kernels  329 us (85%)
  local copies, waits for them, and re-layouts  43.5 us (11%)
  other arithmetic  4.06 us (1%)
    pallas_call x1, Pallas kernels, lead(): pl.pallas_call(lead_kernel, out_shape=(sds((SEQ, D), bf), sds((3 * SEQ, D...  169 us
    pallas_call x1, Pallas kernels, rest(): pl.pallas_call(rest_kernel, out_shape=(sds((SEQ, D), bf), sds((SEQ, D), b...  160 us
    unnamed x15, local copies, waits for them, and re-layouts  14.4 us
    convert_element_type x2, local copies, waits for them, and re-layouts, shards(): dw1 = g[1:8:2].transpose(2, 1, 0, 3).reshape(HF, FF).astype(f32)  11.6 us

profile of v2, /device:TPU:0, one launch (start us, length us, event | category | flops | bytes accessed | tf_op | source)
XLA Modules:
  0.0 378.7 jit_solution(3817322173327375391)
XLA Ops:
  1.3 0.9 dynamic-update-slice
  2.2 0.9 dynamic-update-slice.1
  3.0 0.8 dynamic-update-slice.2
  3.9 0.9 dynamic-update-slice.3
  4.7 0.9 dynamic-update-slice.4
  5.6 0.9 dynamic-update-slice.5
  6.5 0.9 dynamic-update-slice.6
  7.3 0.9 dynamic-update-slice.7
  8.2 0.6 pad_convert_fusion.sm_own
  8.8 168.8 %lead.1 = (bf16[1024,768]{1,0:T(8,128)(2,1)}, bf16[3072,768]{1,0:T(8,128)(2,1)}, bf16[1024,768]{1,0:T(8,128)(2,1)}, bf16[1024,128]{1,0:T(8,128)(2,1)}, bf16[768,...) custom-call(s32[1]{0:T(128)S(6)} %copy.50.len_ref, ...), custom_call_target="tpu_custom_call" | custom-call | flops 7000000000 | bytes 10000000 | tf_op jit(solution)/shard_map/lead/pallas_call | solution.py:584
  177.6 160.5 %rest.1 = (bf16[1024,768]{1,0:T(8,128)(2,1)}, bf16[1024,768]{1,0:T(8,128)(2,1)}, bf16[12,768,384]{2,1,0:T(8,128)(2,1)}, f32[16,768]{1,0:T(8,128)}) custom-call(s32[1]{0:T(128)S(6)} %copy.50.len_ref, f32[2,16,384]{2,1,0:T(8,128)} %get-tuple-element.27.sm_ref, bf16[1024,768]{1,0:T(8,128)(2,1)} %x_any.1, bf16[1024,768]{1,0:T(8,128)(2,1)} %get-tuple-element.28.o_any, ...), custom_call_target="tpu_custom_call" | custom-call | flops 49000001536 | bytes 50000000 | tf_op jit(solution)/shard_map/rest/pallas_call | solution.py:862
  338.1 1.6 dynamic-slice_reduce_fusion.1
  339.7 0.7 dynamic-slice.5
  340.4 0.6 reshape.59
  341.0 0.7 slice.44
  341.8 0.6 dynamic-slice_reduce_fusion
  342.4 3.4 convert_bitcast_fusion
  345.8 3.6 copy.36
  349.4 2.5 copy.39
  351.9 5.3 %copy.35 = f32[384,2,4,384]{3,2,1,0:T(4,128)} copy(f32[384,2,4,384]{3,0,1,2:T(8,128)S(1)} %get-tuple-element.61) | data formatting | bytes 9437184 | tf_op jit(solution)/shard_map/convert_element_type | solution.py:897
  357.2 6.4 %reshape.62 = f32[384,3072]{1,0:T(8,128)} reshape(f32[384,2,4,384]{3,2,1,0:T(4,128)} %copy.35) | data formatting | bytes 9437184 | tf_op jit(solution)/shard_map/convert_element_type | solution.py:897
  363.5 1.7 slice.42
  365.2 2.6 copy.32
  367.8 2.2 copy.33
  370.1 2.9 copy.37
  373.0 1.1 slice.45
  374.1 0.0 copy-start.1
  374.1 0.1 convert_bitcast_fusion.2
  374.2 0.0 copy-start
  374.2 1.1 copy.38
  375.3 0.6 copy-done.1
  376.0 1.1 copy.51
  377.1 0.0 copy-done
  377.1 1.1 copy.52
  (2 shorter events, 0.0 us)
Async XLA Ops:
  374.1 1.8 copy-start.1
  374.2 2.9 copy-start
